TPU v7x, 256 devices: a whole 4x4x8 slice. The times are simulated.
256 devices in a mesh: section: 8 (over z), cp: 32 (over y, x, core).
Axes of the slice: x: 4, y: 4, z: 8, core: 2. Of those that a mesh axis runs over, the one named last changes fastest.
Arguments:
- inputs: bfloat16 [2, 5120, 2048], P(None, 'cp'), may hold values from -6 to 6
- norm_gain: float32 [8, 2048], P('section'), may hold values from 0.1 to 1.9
- qkv_weight: bfloat16 [8, 2048, 3072], P('section', 'cp')
- batch_lengths: int32 [2], replicated, may hold values from 2560 to 5120, as said below
- doc_lengths: int32 [2, 128], replicated, may hold values from 1 to 160, 5120 in all within a row
- doc_shift: int32 [2, 128], replicated, may hold values 0 or 1
Outputs:
- section_out: bfloat16 [8, 2, 10240, 2048], P('section', None, 'cp')
Inputs may be any that keep to these rules, and one draw needn't show every extreme that they name: `batch_lengths`: one micro-batch in every draw holds all 5120 rows. `doc_lengths`: the lengths of a micro-batch sum to 5120.
All inputs are finite; a program needn't handle non-finite values.
Results may differ from a plain program's by a relative error of at most 0.015.
Values may be sent and summed in bfloat16 or wider, within the bound.
A program may use at most 64 MiB of HBM per device.

v0:
```python
import math

import jax
import jax.numpy as jnp
from jax import lax
from jax.sharding import PartitionSpec as P

KVHEADS = 4
HEAD_DIM = 128


EPSILON = 1e-05
NEGATIVE = -1e30


def passed_along(value, axis, steps):
    count = lax.axis_size(axis)
    first, last = (max(0, -steps), min(count, count - steps))
    return lax.ppermute(value, axis, [(source, source + steps) for source in range(first, last)])


def project(state, gains, weights):
    values = state.astype(jnp.float32)
    inverse = lax.rsqrt(jnp.mean(values * values, axis=1, keepdims=True) + EPSILON)
    normed = (values * inverse * gains[None, :]).astype(jnp.bfloat16)
    return jnp.dot(normed, weights, preferred_element_type=jnp.float32).astype(jnp.bfloat16)


def split_heads(projected, model_width, kv_heads, head_size):
    row_count = projected.shape[0]
    group_size = model_width // head_size // kv_heads
    queries = projected[:, :model_width].reshape(row_count, kv_heads, group_size, head_size)
    key_rows = projected[:, model_width : model_width + kv_heads * head_size].reshape(
        row_count, kv_heads, head_size
    )
    val_rows = projected[:, model_width + kv_heads * head_size :].reshape(
        row_count, kv_heads, head_size
    )
    return (queries, key_rows, val_rows)


def mix(queries, key_rows, val_rows, query_docs, key_docs, query_places, key_places, key_living):
    head_size = queries.shape[3]
    scores = jnp.einsum(
        "ikgd,jkd->kgij", queries, key_rows, preferred_element_type=jnp.float32
    ) / math.sqrt(head_size)
    same_place = key_places[None, :] == query_places[:, None]
    allowed = (
        (query_docs[:, None] == key_docs[None, :])
        & (key_places[None, :] <= query_places[:, None])
        & (key_living[None, :] | same_place)
    )
    scores = jnp.where(allowed, scores, NEGATIVE)
    highest = jnp.max(scores, axis=3, keepdims=True)
    weighted = jnp.where(allowed, jnp.exp(scores - highest), 0.0)
    totals = jnp.sum(weighted, axis=3, keepdims=True)
    shares = (weighted / totals).astype(jnp.bfloat16)
    mixture = jnp.einsum("kgij,jkd->ikgd", shares, val_rows, preferred_element_type=jnp.float32)
    return mixture.reshape(queries.shape[0], -1)


def pick(array, chosen):
    return lax.dynamic_index_in_dim(array, chosen, 0, keepdims=False)


def shards(inputs, norm_gain, qkv_weight, batch_lengths, doc_lengths, doc_shift):
    context_size = lax.axis_size("cp")
    context_rank = lax.axis_index("cp")
    sections = lax.axis_size("section")
    section_id = lax.axis_index("section")
    batches = inputs.shape[0]
    row_count = inputs.shape[1]
    model_width = inputs.shape[2]
    kv_heads = KVHEADS
    head_size = HEAD_DIM
    weights = lax.all_gather(qkv_weight[0], "cp", axis=0, tiled=True)
    norm_gains = norm_gain[0]
    offsets = jnp.arange(2 * row_count, dtype=jnp.int32)
    places = (context_rank - 1) * row_count + offsets
    doc_list, living_list, present_list, outgoing_list = ([], [], [], [])
    for batch_index in range(batches):
        lengths = doc_lengths[batch_index]
        ends = jnp.cumsum(lengths)
        starts = ends - lengths
        first_rank = starts // row_count
        last_rank = (ends - 1) // row_count
        movable = ((first_rank == last_rank) & (last_rank < context_size - 1)).astype(jnp.int32)
        target_doc = last_rank + doc_shift[batch_index] * movable
        doc_ids = jnp.sum((starts[None, :] <= places[:, None]).astype(jnp.int32), axis=1) - 1
        matches = doc_ids[:, None] == jnp.arange(lengths.shape[0], dtype=jnp.int32)[None, :]
        target_slot = jnp.sum(jnp.where(matches, target_doc[None, :], 0), axis=1)
        present = (places >= 0) & (places < batch_lengths[batch_index])
        living = present & (target_slot == context_rank)
        outgoing = present[row_count:] & (target_slot[row_count:] == context_rank + 1)
        doc_list.append(doc_ids)
        living_list.append(living)
        present_list.append(present)
        outgoing_list.append(outgoing)
    doc_all = jnp.stack(doc_list)
    living_all = jnp.stack(living_list)
    outgoing_all = jnp.stack(outgoing_list)
    steps_total = sections + batches - 1

    def layer(buffer, doc_ids, living):
        projected = project(buffer, norm_gains, weights)
        queries, key_rows, val_rows = split_heads(projected, model_width, kv_heads, head_size)
        mixture = mix(queries, key_rows, val_rows, doc_ids, doc_ids, places, places, living)
        return jnp.where(living[:, None], buffer.astype(jnp.float32) + mixture, 0.0).astype(
            jnp.bfloat16
        )

    def skipped(buffer, doc_ids, living):
        return jnp.zeros_like(buffer)

    def plan(moment):
        slot_batch = moment - section_id
        active = (slot_batch >= 0) & (slot_batch < batches)
        chosen = jnp.clip(slot_batch, 0, batches - 1)
        return (active, chosen)

    def store(collected, result, active, chosen):
        updated = lax.dynamic_update_index_in_dim(collected, result, chosen, 0)
        return jnp.where(active, updated, collected)

    collected_init = jnp.zeros((batches, 2 * row_count, model_width), jnp.bfloat16)

    def advance(moment, carry):
        incoming, collected = carry
        active, chosen = plan(moment)
        doc_now = pick(doc_all, chosen)
        living_now = pick(living_all, chosen)
        outgoing_now = pick(outgoing_all, chosen)
        home_rows = jnp.where(section_id == 0, pick(inputs, chosen), incoming)
        sending = jnp.where(outgoing_now[:, None], home_rows, 0)
        arrived = passed_along(sending, "cp", 1)
        buffer = jnp.where(living_now[:, None], jnp.concatenate([arrived, home_rows], axis=0), 0)
        result = lax.cond(active, layer, skipped, buffer, doc_now, living_now)
        collected = store(collected, result, active, chosen)
        returned = passed_along(result[:row_count], "cp", -1)
        home_next = jnp.where(living_now[row_count:, None], result[row_count:], returned)
        passed = passed_along(home_next, "section", 1)
        return (passed, collected)

    start_rows = jnp.zeros((row_count, model_width), jnp.bfloat16)
    final_rows, collected = lax.fori_loop(0, steps_total, advance, (start_rows, collected_init))
    return collected[None]


def solution(mesh):
    placed = (P(None, "cp", None), P("section", None), P("section", "cp", None), P(), P(), P())
    return jax.shard_map(
        shards,
        mesh=mesh,
        in_specs=placed,
        out_specs=P("section", None, "cp", None),
        check_vma=False,
    )
```

profile of v0, /device:TPU:240, one launch (start us, length us, event | category | flops | bytes accessed | tf_op | source)
XLA Modules:
  0.0 800.2 jit_solution(5653473574693394697)
XLA Ops:
  14.5 63.3 %all-gather.3.cloned.1.call-done = bf16[1,2048,3072]{2,1,0:T(8,128)(2,1)} async-done(((bf16[1,64,3072]{2,1,0:T(8,128)(2,1)}), bf16[1,2048,3072]{2,1,0:T(8,128)(2,1)}) %all-gather.3.cloned.1.call-update) | async-done | bytes 12582928 | tf_op jit(solution)/shard_map/all_gather | solution.py:76
  80.6 712.8 %while.18 = (s32[]{:T(128)}, bf16[160,2048]{1,0:T(8,128)(2,1)}, bf16[2,320,2048]{2,1,0:T(8,128)(2,1)}, s32[]{:T(128)}, pred[2,320]{1,0:T(4,128)(4,1)S(1)}, /*ind...) while((s32[]{:T(128)}, bf16[160,2048]{1,0:T(8,128)(2,1)}, ...), condition=%wide.region_12.13_spmd.clone, body=%wide.region_6.12_spmd.clone.sunk | while | flops 4895171584 | bytes 92153976 | solution.py:145
  82.0 2.2 collective-permute-start
  84.2 11.8 %collective-permute-done = bf16[160,2048]{1,0:T(8,128)(2,1)S(1)} collective-permute-done((bf16[160,2048]{1,0:T(8,128)(2,1)S(1)}, bf16[160,2048]{1,0:T(8,128)(2,1)S(1)}, u32[]{:S(2)}, u32[]{:S(2)}) %collective-permute-start) | collective-permute-done | bytes 655392 | tf_op jit(solution)/shard_map/while/body/eval_jaxpr/ppermute | solution.py:19
  96.4 1.9 collective-permute-start.1
  98.4 8.0 collective-permute-done.1
  107.9 2.9 fusion.40
  110.7 12.8 %collective-permute-done.2 = bf16[160,2048]{1,0:T(8,128)(2,1)} collective-permute-done((bf16[160,2048]{1,0:T(8,128)(2,1)S(1)}, bf16[160,2048]{1,0:T(8,128)(2,1)}, u32[]{:S(2)}, u32[]{:S(2)}) %collective-permute-start.2) | collective-permute-done | bytes 655392 | tf_op jit(solution)/shard_map/while/body/eval_jaxpr/ppermute | solution.py:19
  125.0 1.9 collective-permute-start
  126.9 12.1 %collective-permute-done = bf16[160,2048]{1,0:T(8,128)(2,1)S(1)} collective-permute-done((bf16[160,2048]{1,0:T(8,128)(2,1)S(1)}, bf16[160,2048]{1,0:T(8,128)(2,1)S(1)}, u32[]{:S(2)}, u32[]{:S(2)}) %collective-permute-start) | collective-permute-done | bytes 655392 | tf_op jit(solution)/shard_map/while/body/eval_jaxpr/ppermute | solution.py:19
  141.4 8.0 collective-permute-done.1
  150.8 2.9 fusion.40
  153.7 12.7 %collective-permute-done.2 = bf16[160,2048]{1,0:T(8,128)(2,1)} collective-permute-done((bf16[160,2048]{1,0:T(8,128)(2,1)S(1)}, bf16[160,2048]{1,0:T(8,128)(2,1)}, u32[]{:S(2)}, u32[]{:S(2)}) %collective-permute-start.2) | collective-permute-done | bytes 655392 | tf_op jit(solution)/shard_map/while/body/eval_jaxpr/ppermute | solution.py:19
  167.8 1.9 collective-permute-start
  169.8 12.1 %collective-permute-done = bf16[160,2048]{1,0:T(8,128)(2,1)S(1)} collective-permute-done((bf16[160,2048]{1,0:T(8,128)(2,1)S(1)}, bf16[160,2048]{1,0:T(8,128)(2,1)S(1)}, u32[]{:S(2)}, u32[]{:S(2)}) %collective-permute-start) | collective-permute-done | bytes 655392 | tf_op jit(solution)/shard_map/while/body/eval_jaxpr/ppermute | solution.py:19
  182.2 1.9 collective-permute-start.1
  184.2 8.0 collective-permute-done.1
  193.7 2.9 fusion.40
  196.5 12.3 %collective-permute-done.2 = bf16[160,2048]{1,0:T(8,128)(2,1)} collective-permute-done((bf16[160,2048]{1,0:T(8,128)(2,1)S(1)}, bf16[160,2048]{1,0:T(8,128)(2,1)}, u32[]{:S(2)}, u32[]{:S(2)}) %collective-permute-start.2) | collective-permute-done | bytes 655392 | tf_op jit(solution)/shard_map/while/body/eval_jaxpr/ppermute | solution.py:19
  212.3 12.1 %collective-permute-done = bf16[160,2048]{1,0:T(8,128)(2,1)S(1)} collective-permute-done((bf16[160,2048]{1,0:T(8,128)(2,1)S(1)}, bf16[160,2048]{1,0:T(8,128)(2,1)S(1)}, u32[]{:S(2)}, u32[]{:S(2)}) %collective-permute-start) | collective-permute-done | bytes 655392 | tf_op jit(solution)/shard_map/while/body/eval_jaxpr/ppermute | solution.py:19
  226.8 8.0 collective-permute-done.1
  236.2 2.9 fusion.40
  239.0 11.8 %collective-permute-done.2 = bf16[160,2048]{1,0:T(8,128)(2,1)} collective-permute-done((bf16[160,2048]{1,0:T(8,128)(2,1)S(1)}, bf16[160,2048]{1,0:T(8,128)(2,1)}, u32[]{:S(2)}, u32[]{:S(2)}) %collective-permute-start.2) | collective-permute-done | bytes 655392 | tf_op jit(solution)/shard_map/while/body/eval_jaxpr/ppermute | solution.py:19
  254.3 12.1 %collective-permute-done = bf16[160,2048]{1,0:T(8,128)(2,1)S(1)} collective-permute-done((bf16[160,2048]{1,0:T(8,128)(2,1)S(1)}, bf16[160,2048]{1,0:T(8,128)(2,1)S(1)}, u32[]{:S(2)}, u32[]{:S(2)}) %collective-permute-start) | collective-permute-done | bytes 655392 | tf_op jit(solution)/shard_map/while/body/eval_jaxpr/ppermute | solution.py:19
  268.8 8.0 collective-permute-done.1
  278.2 2.9 fusion.40
  281.0 11.2 %collective-permute-done.2 = bf16[160,2048]{1,0:T(8,128)(2,1)} collective-permute-done((bf16[160,2048]{1,0:T(8,128)(2,1)S(1)}, bf16[160,2048]{1,0:T(8,128)(2,1)}, u32[]{:S(2)}, u32[]{:S(2)}) %collective-permute-start.2) | collective-permute-done | bytes 655392 | tf_op jit(solution)/shard_map/while/body/eval_jaxpr/ppermute | solution.py:19
  295.6 12.1 %collective-permute-done = bf16[160,2048]{1,0:T(8,128)(2,1)S(1)} collective-permute-done((bf16[160,2048]{1,0:T(8,128)(2,1)S(1)}, bf16[160,2048]{1,0:T(8,128)(2,1)S(1)}, u32[]{:S(2)}, u32[]{:S(2)}) %collective-permute-start) | collective-permute-done | bytes 655392 | tf_op jit(solution)/shard_map/while/body/eval_jaxpr/ppermute | solution.py:19
  310.1 8.0 collective-permute-done.1
  319.5 2.9 fusion.40
  322.4 12.6 %collective-permute-done.2 = bf16[160,2048]{1,0:T(8,128)(2,1)} collective-permute-done((bf16[160,2048]{1,0:T(8,128)(2,1)S(1)}, bf16[160,2048]{1,0:T(8,128)(2,1)}, u32[]{:S(2)}, u32[]{:S(2)}) %collective-permute-start.2) | collective-permute-done | bytes 655392 | tf_op jit(solution)/shard_map/while/body/eval_jaxpr/ppermute | solution.py:19
  336.5 1.9 collective-permute-start
  338.4 12.1 %collective-permute-done = bf16[160,2048]{1,0:T(8,128)(2,1)S(1)} collective-permute-done((bf16[160,2048]{1,0:T(8,128)(2,1)S(1)}, bf16[160,2048]{1,0:T(8,128)(2,1)S(1)}, u32[]{:S(2)}, u32[]{:S(2)}) %collective-permute-start) | collective-permute-done | bytes 655392 | tf_op jit(solution)/shard_map/while/body/eval_jaxpr/ppermute | solution.py:19
  350.9 1.9 collective-permute-start.1
  352.9 8.0 collective-permute-done.1
  362.3 2.9 fusion.40
  365.2 268.7 %collective-permute-done.2 = bf16[160,2048]{1,0:T(8,128)(2,1)} collective-permute-done((bf16[160,2048]{1,0:T(8,128)(2,1)S(1)}, bf16[160,2048]{1,0:T(8,128)(2,1)}, u32[]{:S(2)}, u32[]{:S(2)}) %collective-permute-start.2) | collective-permute-done | bytes 655392 | tf_op jit(solution)/shard_map/while/body/eval_jaxpr/ppermute | solution.py:19
  635.3 1.9 collective-permute-start
  637.3 14.5 %collective-permute-done = bf16[160,2048]{1,0:T(8,128)(2,1)S(1)} collective-permute-done((bf16[160,2048]{1,0:T(8,128)(2,1)S(1)}, bf16[160,2048]{1,0:T(8,128)(2,1)S(1)}, u32[]{:S(2)}, u32[]{:S(2)}) %collective-permute-start) | collective-permute-done | bytes 655392 | tf_op jit(solution)/shard_map/while/body/eval_jaxpr/ppermute | solution.py:19
  652.0 38.8 %conditional.3 = (bf16[320,2048]{1,0:T(8,128)(2,1)S(1)}) conditional(s32[]{:T(128)} %convert_element_type.82, () %tuple.67, (pred[1,320]{1,0:T(4,128)(4,1)S(1)}, bf16[320,2048]{1,0:T(8,128)(2,1)S(1)}, f32[1,2048]{1,0:T(1,128)S(1)}, bf16[2048,3072]{1,0:T(8,128)(2,1)}, s32[2,320]{1,0:T(2,128)S(1)}, /*index=5*/s32[]{:T(128)}, s32[]{:T(128)}, ...), branch_computations={%region_7.7_spmd, %region_8.11_spmd} | conditional | flops 4890911744 | bytes 71834000 | solution.py:137
  652.5 10.3 %convolution_convert_fusion = bf16[320,3072]{1,0:T(8,128)(2,1)} fusion(bf16[2048,3072]{1,0:T(8,128)(2,1)} %get-tuple-element.331, f32[2048]{0:T(1024)S(1)} %bitcast.67, f32[320]{0:T(512)S(1)} %add_rsqrt_fusion, bf16[320,2048]{1,0:T(8,128)(2,1)S(1)} %get-tuple-element.329, pred[320]{0:T(512)(128)(4,1)S(1)} %reduce), kind=kOutput, calls=%fused_computation.6 | convolution fusion | flops 4030791680 | bytes 15869504 | tf_op jit(solution)/shard_map/while/body/eval_jaxpr/cond/branch_1_fun/dot_general | solution.py:26
  664.1 2.5 slice.91
  666.6 3.2 reshape.208
  671.3 4.9 fusion.36
  676.3 4.7 fusion.13
  681.1 3.2 copy.24
  684.3 4.1 reshape.209
  688.4 2.4 fusion.12
  692.9 8.0 collective-permute-done.1
  702.3 2.9 fusion.40
  705.1 9.2 %collective-permute-done.2 = bf16[160,2048]{1,0:T(8,128)(2,1)} collective-permute-done((bf16[160,2048]{1,0:T(8,128)(2,1)S(1)}, bf16[160,2048]{1,0:T(8,128)(2,1)}, u32[]{:S(2)}, u32[]{:S(2)}) %collective-permute-start.2) | collective-permute-done | bytes 655392 | tf_op jit(solution)/shard_map/while/body/eval_jaxpr/ppermute | solution.py:19
  717.7 13.8 %collective-permute-done = bf16[160,2048]{1,0:T(8,128)(2,1)S(1)} collective-permute-done((bf16[160,2048]{1,0:T(8,128)(2,1)S(1)}, bf16[160,2048]{1,0:T(8,128)(2,1)S(1)}, u32[]{:S(2)}, u32[]{:S(2)}) %collective-permute-start) | collective-permute-done | bytes 655392 | tf_op jit(solution)/shard_map/while/body/eval_jaxpr/ppermute | solution.py:19
  731.6 38.8 %conditional.3 = (bf16[320,2048]{1,0:T(8,128)(2,1)S(1)}) conditional(s32[]{:T(128)} %convert_element_type.82, () %tuple.67, (pred[1,320]{1,0:T(4,128)(4,1)S(1)}, bf16[320,2048]{1,0:T(8,128)(2,1)S(1)}, f32[1,2048]{1,0:T(1,128)S(1)}, bf16[2048,3072]{1,0:T(8,128)(2,1)}, s32[2,320]{1,0:T(2,128)S(1)}, /*index=5*/s32[]{:T(128)}, s32[]{:T(128)}, ...), branch_computations={%region_7.7_spmd, %region_8.11_spmd} | conditional | flops 4890911744 | bytes 71834000 | solution.py:137
  732.2 10.3 %convolution_convert_fusion = bf16[320,3072]{1,0:T(8,128)(2,1)} fusion(bf16[2048,3072]{1,0:T(8,128)(2,1)} %get-tuple-element.331, f32[2048]{0:T(1024)S(1)} %bitcast.67, f32[320]{0:T(512)S(1)} %add_rsqrt_fusion, bf16[320,2048]{1,0:T(8,128)(2,1)S(1)} %get-tuple-element.329, pred[320]{0:T(512)(128)(4,1)S(1)} %reduce), kind=kOutput, calls=%fused_computation.6 | convolution fusion | flops 4030791680 | bytes 15869504 | tf_op jit(solution)/shard_map/while/body/eval_jaxpr/cond/branch_1_fun/dot_general | solution.py:26
  743.7 2.5 slice.91
  746.3 3.2 reshape.208
  751.0 4.9 fusion.36
  756.0 4.7 fusion.13
  760.7 3.2 copy.24
  763.9 4.1 reshape.209
  768.0 2.4 fusion.12
  772.5 8.0 collective-permute-done.1
  781.9 2.9 fusion.40
  784.8 8.6 %collective-permute-done.2 = bf16[160,2048]{1,0:T(8,128)(2,1)} collective-permute-done((bf16[160,2048]{1,0:T(8,128)(2,1)S(1)}, bf16[160,2048]{1,0:T(8,128)(2,1)}, u32[]{:S(2)}, u32[]{:S(2)}) %collective-permute-start.2) | collective-permute-done | bytes 655392 | tf_op jit(solution)/shard_map/while/body/eval_jaxpr/ppermute | solution.py:19
  (159 shorter events, 67.1 us)
Async XLA Ops:
  6.5 74.0 %copy-start = (f32[1,2048]{1,0:T(1,128)S(1)}, f32[1,2048]{1,0:T(1,128)}, u32[]{:S(2)}) copy-start(f32[1,2048]{1,0:T(1,128)} %param.11) | copy-start | bytes 24580
  6.5 71.3 %all-gather.3.cloned.1.call-start = ((), (), s32[]{:S(2)}) async-start(), calls=%async_computation | async-start | bytes 12976128 | tf_op jit(solution)/shard_map/all_gather | solution.py:76
  82.0 14.0 %collective-permute-start = (bf16[160,2048]{1,0:T(8,128)(2,1)S(1)}, bf16[160,2048]{1,0:T(8,128)(2,1)S(1)}, u32[]{:S(2)}, u32[]{:S(2)}) collective-permute-start(bf16[160,2048]{1,0:T(8,128)(2,1)S(1)} %get-tuple-element.500), channel_id=1, source_target_pairs={{0,1},{1,2},{2,3},{3,4},{4,5},{5,6},{6,7},{7,8},{8,9},{9,10},{10,1... | collective-permute-start | bytes 1966088 | tf_op jit(solution)/shard_map/while/body/eval_jaxpr/ppermute | solution.py:19
  96.4 10.0 %collective-permute-start.1 = (bf16[160,2048]{1,0:T(8,128)(2,1)S(1)}, bf16[160,2048]{1,0:T(8,128)(2,1)S(1)}, u32[]{:S(2)}, u32[]{:S(2)}) collective-permute-start(bf16[160,2048]{1,0:T(8,128)(2,1)S(1)} %slice.124), channel_id=1, source_target_pairs={{1,0},{2,1},{3,2},{4,3},{5,4},{6,5},{7,6},{8,7},{9,8},{10,9},{11,1... | collective-permute-start | bytes 1966088 | tf_op jit(solution)/shard_map/while/body/eval_jaxpr/ppermute | solution.py:19
  106.6 17.0 %collective-permute-start.2 = (bf16[160,2048]{1,0:T(8,128)(2,1)S(1)}, bf16[160,2048]{1,0:T(8,128)(2,1)}, u32[]{:S(2)}, u32[]{:S(2)}) collective-permute-start(bf16[160,2048]{1,0:T(8,128)(2,1)S(1)} %slice_select_fusion.2), channel_id=1, source_target_pairs={{0,32},{32,64},{64,96},{96,128},{128,160},{160,192},{192,224},{1,3... | collective-permute-start | bytes 1966088 | tf_op jit(solution)/shard_map/while/body/eval_jaxpr/ppermute | solution.py:19
  125.0 14.0 %collective-permute-start = (bf16[160,2048]{1,0:T(8,128)(2,1)S(1)}, bf16[160,2048]{1,0:T(8,128)(2,1)S(1)}, u32[]{:S(2)}, u32[]{:S(2)}) collective-permute-start(bf16[160,2048]{1,0:T(8,128)(2,1)S(1)} %get-tuple-element.500), channel_id=1, source_target_pairs={{0,1},{1,2},{2,3},{3,4},{4,5},{5,6},{6,7},{7,8},{8,9},{9,10},{10,1... | collective-permute-start | bytes 1966088 | tf_op jit(solution)/shard_map/while/body/eval_jaxpr/ppermute | solution.py:19
  139.4 10.0 %collective-permute-start.1 = (bf16[160,2048]{1,0:T(8,128)(2,1)S(1)}, bf16[160,2048]{1,0:T(8,128)(2,1)S(1)}, u32[]{:S(2)}, u32[]{:S(2)}) collective-permute-start(bf16[160,2048]{1,0:T(8,128)(2,1)S(1)} %slice.124), channel_id=1, source_target_pairs={{1,0},{2,1},{3,2},{4,3},{5,4},{6,5},{7,6},{8,7},{9,8},{10,9},{11,1... | collective-permute-start | bytes 1966088 | tf_op jit(solution)/shard_map/while/body/eval_jaxpr/ppermute | solution.py:19
  149.5 16.8 %collective-permute-start.2 = (bf16[160,2048]{1,0:T(8,128)(2,1)S(1)}, bf16[160,2048]{1,0:T(8,128)(2,1)}, u32[]{:S(2)}, u32[]{:S(2)}) collective-permute-start(bf16[160,2048]{1,0:T(8,128)(2,1)S(1)} %slice_select_fusion.2), channel_id=1, source_target_pairs={{0,32},{32,64},{64,96},{96,128},{128,160},{160,192},{192,224},{1,3... | collective-permute-start | bytes 1966088 | tf_op jit(solution)/shard_map/while/body/eval_jaxpr/ppermute | solution.py:19
  167.8 14.0 %collective-permute-start = (bf16[160,2048]{1,0:T(8,128)(2,1)S(1)}, bf16[160,2048]{1,0:T(8,128)(2,1)S(1)}, u32[]{:S(2)}, u32[]{:S(2)}) collective-permute-start(bf16[160,2048]{1,0:T(8,128)(2,1)S(1)} %get-tuple-element.500), channel_id=1, source_target_pairs={{0,1},{1,2},{2,3},{3,4},{4,5},{5,6},{6,7},{7,8},{8,9},{9,10},{10,1... | collective-permute-start | bytes 1966088 | tf_op jit(solution)/shard_map/while/body/eval_jaxpr/ppermute | solution.py:19
  182.2 10.0 %collective-permute-start.1 = (bf16[160,2048]{1,0:T(8,128)(2,1)S(1)}, bf16[160,2048]{1,0:T(8,128)(2,1)S(1)}, u32[]{:S(2)}, u32[]{:S(2)}) collective-permute-start(bf16[160,2048]{1,0:T(8,128)(2,1)S(1)} %slice.124), channel_id=1, source_target_pairs={{1,0},{2,1},{3,2},{4,3},{5,4},{6,5},{7,6},{8,7},{9,8},{10,9},{11,1... | collective-permute-start | bytes 1966088 | tf_op jit(solution)/shard_map/while/body/eval_jaxpr/ppermute | solution.py:19
  192.4 16.5 %collective-permute-start.2 = (bf16[160,2048]{1,0:T(8,128)(2,1)S(1)}, bf16[160,2048]{1,0:T(8,128)(2,1)}, u32[]{:S(2)}, u32[]{:S(2)}) collective-permute-start(bf16[160,2048]{1,0:T(8,128)(2,1)S(1)} %slice_select_fusion.2), channel_id=1, source_target_pairs={{0,32},{32,64},{64,96},{96,128},{128,160},{160,192},{192,224},{1,3... | collective-permute-start | bytes 1966088 | tf_op jit(solution)/shard_map/while/body/eval_jaxpr/ppermute | solution.py:19
  210.3 14.0 %collective-permute-start = (bf16[160,2048]{1,0:T(8,128)(2,1)S(1)}, bf16[160,2048]{1,0:T(8,128)(2,1)S(1)}, u32[]{:S(2)}, u32[]{:S(2)}) collective-permute-start(bf16[160,2048]{1,0:T(8,128)(2,1)S(1)} %get-tuple-element.500), channel_id=1, source_target_pairs={{0,1},{1,2},{2,3},{3,4},{4,5},{5,6},{6,7},{7,8},{8,9},{9,10},{10,1... | collective-permute-start | bytes 1966088 | tf_op jit(solution)/shard_map/while/body/eval_jaxpr/ppermute | solution.py:19
  224.7 10.0 %collective-permute-start.1 = (bf16[160,2048]{1,0:T(8,128)(2,1)S(1)}, bf16[160,2048]{1,0:T(8,128)(2,1)S(1)}, u32[]{:S(2)}, u32[]{:S(2)}) collective-permute-start(bf16[160,2048]{1,0:T(8,128)(2,1)S(1)} %slice.124), channel_id=1, source_target_pairs={{1,0},{2,1},{3,2},{4,3},{5,4},{6,5},{7,6},{8,7},{9,8},{10,9},{11,1... | collective-permute-start | bytes 1966088 | tf_op jit(solution)/shard_map/while/body/eval_jaxpr/ppermute | solution.py:19
  234.9 16.0 %collective-permute-start.2 = (bf16[160,2048]{1,0:T(8,128)(2,1)S(1)}, bf16[160,2048]{1,0:T(8,128)(2,1)}, u32[]{:S(2)}, u32[]{:S(2)}) collective-permute-start(bf16[160,2048]{1,0:T(8,128)(2,1)S(1)} %slice_select_fusion.2), channel_id=1, source_target_pairs={{0,32},{32,64},{64,96},{96,128},{128,160},{160,192},{192,224},{1,3... | collective-permute-start | bytes 1966088 | tf_op jit(solution)/shard_map/while/body/eval_jaxpr/ppermute | solution.py:19
  252.3 14.0 %collective-permute-start = (bf16[160,2048]{1,0:T(8,128)(2,1)S(1)}, bf16[160,2048]{1,0:T(8,128)(2,1)S(1)}, u32[]{:S(2)}, u32[]{:S(2)}) collective-permute-start(bf16[160,2048]{1,0:T(8,128)(2,1)S(1)} %get-tuple-element.500), channel_id=1, source_target_pairs={{0,1},{1,2},{2,3},{3,4},{4,5},{5,6},{6,7},{7,8},{8,9},{9,10},{10,1... | collective-permute-start | bytes 1966088 | tf_op jit(solution)/shard_map/while/body/eval_jaxpr/ppermute | solution.py:19
  266.7 10.0 %collective-permute-start.1 = (bf16[160,2048]{1,0:T(8,128)(2,1)S(1)}, bf16[160,2048]{1,0:T(8,128)(2,1)S(1)}, u32[]{:S(2)}, u32[]{:S(2)}) collective-permute-start(bf16[160,2048]{1,0:T(8,128)(2,1)S(1)} %slice.124), channel_id=1, source_target_pairs={{1,0},{2,1},{3,2},{4,3},{5,4},{6,5},{7,6},{8,7},{9,8},{10,9},{11,1... | collective-permute-start | bytes 1966088 | tf_op jit(solution)/shard_map/while/body/eval_jaxpr/ppermute | solution.py:19
  276.9 15.4 %collective-permute-start.2 = (bf16[160,2048]{1,0:T(8,128)(2,1)S(1)}, bf16[160,2048]{1,0:T(8,128)(2,1)}, u32[]{:S(2)}, u32[]{:S(2)}) collective-permute-start(bf16[160,2048]{1,0:T(8,128)(2,1)S(1)} %slice_select_fusion.2), channel_id=1, source_target_pairs={{0,32},{32,64},{64,96},{96,128},{128,160},{160,192},{192,224},{1,3... | collective-permute-start | bytes 1966088 | tf_op jit(solution)/shard_map/while/body/eval_jaxpr/ppermute | solution.py:19
  293.7 14.0 %collective-permute-start = (bf16[160,2048]{1,0:T(8,128)(2,1)S(1)}, bf16[160,2048]{1,0:T(8,128)(2,1)S(1)}, u32[]{:S(2)}, u32[]{:S(2)}) collective-permute-start(bf16[160,2048]{1,0:T(8,128)(2,1)S(1)} %get-tuple-element.500), channel_id=1, source_target_pairs={{0,1},{1,2},{2,3},{3,4},{4,5},{5,6},{6,7},{7,8},{8,9},{9,10},{10,1... | collective-permute-start | bytes 1966088 | tf_op jit(solution)/shard_map/while/body/eval_jaxpr/ppermute | solution.py:19
  308.1 10.0 %collective-permute-start.1 = (bf16[160,2048]{1,0:T(8,128)(2,1)S(1)}, bf16[160,2048]{1,0:T(8,128)(2,1)S(1)}, u32[]{:S(2)}, u32[]{:S(2)}) collective-permute-start(bf16[160,2048]{1,0:T(8,128)(2,1)S(1)} %slice.124), channel_id=1, source_target_pairs={{1,0},{2,1},{3,2},{4,3},{5,4},{6,5},{7,6},{8,7},{9,8},{10,9},{11,1... | collective-permute-start | bytes 1966088 | tf_op jit(solution)/shard_map/while/body/eval_jaxpr/ppermute | solution.py:19
  318.2 16.8 %collective-permute-start.2 = (bf16[160,2048]{1,0:T(8,128)(2,1)S(1)}, bf16[160,2048]{1,0:T(8,128)(2,1)}, u32[]{:S(2)}, u32[]{:S(2)}) collective-permute-start(bf16[160,2048]{1,0:T(8,128)(2,1)S(1)} %slice_select_fusion.2), channel_id=1, source_target_pairs={{0,32},{32,64},{64,96},{96,128},{128,160},{160,192},{192,224},{1,3... | collective-permute-start | bytes 1966088 | tf_op jit(solution)/shard_map/while/body/eval_jaxpr/ppermute | solution.py:19
  336.5 14.0 %collective-permute-start = (bf16[160,2048]{1,0:T(8,128)(2,1)S(1)}, bf16[160,2048]{1,0:T(8,128)(2,1)S(1)}, u32[]{:S(2)}, u32[]{:S(2)}) collective-permute-start(bf16[160,2048]{1,0:T(8,128)(2,1)S(1)} %get-tuple-element.500), channel_id=1, source_target_pairs={{0,1},{1,2},{2,3},{3,4},{4,5},{5,6},{6,7},{7,8},{8,9},{9,10},{10,1... | collective-permute-start | bytes 1966088 | tf_op jit(solution)/shard_map/while/body/eval_jaxpr/ppermute | solution.py:19
  350.9 10.0 %collective-permute-start.1 = (bf16[160,2048]{1,0:T(8,128)(2,1)S(1)}, bf16[160,2048]{1,0:T(8,128)(2,1)S(1)}, u32[]{:S(2)}, u32[]{:S(2)}) collective-permute-start(bf16[160,2048]{1,0:T(8,128)(2,1)S(1)} %slice.124), channel_id=1, source_target_pairs={{1,0},{2,1},{3,2},{4,3},{5,4},{6,5},{7,6},{8,7},{9,8},{10,9},{11,1... | collective-permute-start | bytes 1966088 | tf_op jit(solution)/shard_map/while/body/eval_jaxpr/ppermute | solution.py:19
  361.0 272.8 %collective-permute-start.2 = (bf16[160,2048]{1,0:T(8,128)(2,1)S(1)}, bf16[160,2048]{1,0:T(8,128)(2,1)}, u32[]{:S(2)}, u32[]{:S(2)}) collective-permute-start(bf16[160,2048]{1,0:T(8,128)(2,1)S(1)} %slice_select_fusion.2), channel_id=1, source_target_pairs={{0,32},{32,64},{64,96},{96,128},{128,160},{160,192},{192,224},{1,3... | collective-permute-start | bytes 1966088 | tf_op jit(solution)/shard_map/while/body/eval_jaxpr/ppermute | solution.py:19
  635.3 16.5 %collective-permute-start = (bf16[160,2048]{1,0:T(8,128)(2,1)S(1)}, bf16[160,2048]{1,0:T(8,128)(2,1)S(1)}, u32[]{:S(2)}, u32[]{:S(2)}) collective-permute-start(bf16[160,2048]{1,0:T(8,128)(2,1)S(1)} %get-tuple-element.500), channel_id=1, source_target_pairs={{0,1},{1,2},{2,3},{3,4},{4,5},{5,6},{6,7},{7,8},{8,9},{9,10},{10,1... | collective-permute-start | bytes 1966088 | tf_op jit(solution)/shard_map/while/body/eval_jaxpr/ppermute | solution.py:19
  690.8 10.0 %collective-permute-start.1 = (bf16[160,2048]{1,0:T(8,128)(2,1)S(1)}, bf16[160,2048]{1,0:T(8,128)(2,1)S(1)}, u32[]{:S(2)}, u32[]{:S(2)}) collective-permute-start(bf16[160,2048]{1,0:T(8,128)(2,1)S(1)} %slice.124), channel_id=1, source_target_pairs={{1,0},{2,1},{3,2},{4,3},{5,4},{6,5},{7,6},{8,7},{9,8},{10,9},{11,1... | collective-permute-start | bytes 1966088 | tf_op jit(solution)/shard_map/while/body/eval_jaxpr/ppermute | solution.py:19
  701.0 13.3 %collective-permute-start.2 = (bf16[160,2048]{1,0:T(8,128)(2,1)S(1)}, bf16[160,2048]{1,0:T(8,128)(2,1)}, u32[]{:S(2)}, u32[]{:S(2)}) collective-permute-start(bf16[160,2048]{1,0:T(8,128)(2,1)S(1)} %slice_select_fusion.2), channel_id=1, source_target_pairs={{0,32},{32,64},{64,96},{96,128},{128,160},{160,192},{192,224},{1,3... | collective-permute-start | bytes 1966088 | tf_op jit(solution)/shard_map/while/body/eval_jaxpr/ppermute | solution.py:19
  715.8 15.7 %collective-permute-start = (bf16[160,2048]{1,0:T(8,128)(2,1)S(1)}, bf16[160,2048]{1,0:T(8,128)(2,1)S(1)}, u32[]{:S(2)}, u32[]{:S(2)}) collective-permute-start(bf16[160,2048]{1,0:T(8,128)(2,1)S(1)} %get-tuple-element.500), channel_id=1, source_target_pairs={{0,1},{1,2},{2,3},{3,4},{4,5},{5,6},{6,7},{7,8},{8,9},{9,10},{10,1... | collective-permute-start | bytes 1966088 | tf_op jit(solution)/shard_map/while/body/eval_jaxpr/ppermute | solution.py:19
  770.5 10.0 %collective-permute-start.1 = (bf16[160,2048]{1,0:T(8,128)(2,1)S(1)}, bf16[160,2048]{1,0:T(8,128)(2,1)S(1)}, u32[]{:S(2)}, u32[]{:S(2)}) collective-permute-start(bf16[160,2048]{1,0:T(8,128)(2,1)S(1)} %slice.124), channel_id=1, source_target_pairs={{1,0},{2,1},{3,2},{4,3},{5,4},{6,5},{7,6},{8,7},{9,8},{10,9},{11,1... | collective-permute-start | bytes 1966088 | tf_op jit(solution)/shard_map/while/body/eval_jaxpr/ppermute | solution.py:19
  780.6 12.8 %collective-permute-start.2 = (bf16[160,2048]{1,0:T(8,128)(2,1)S(1)}, bf16[160,2048]{1,0:T(8,128)(2,1)}, u32[]{:S(2)}, u32[]{:S(2)}) collective-permute-start(bf16[160,2048]{1,0:T(8,128)(2,1)S(1)} %slice_select_fusion.2), channel_id=1, source_target_pairs={{0,32},{32,64},{64,96},{96,128},{128,160},{160,192},{192,224},{1,3... | collective-permute-start | bytes 1966088 | tf_op jit(solution)/shard_map/while/body/eval_jaxpr/ppermute | solution.py:19
Sparse Core Ops, SparseCore 0:
  9.9 67.8 all-gather.2
where the time goes:
time: 808 us; the launch traced here: 800 us
  waiting for transfers between devices  608 us (75%)
  other arithmetic  61.9 us (8%)
  starting transfers between devices  46.4 us (6%)
  local copies, waits for them, and re-layouts  36.6 us (5%)
  matrix products  32.5 us (4%)
  between operations  13.5 us (2%)
    ppermute x27, waiting for transfers between devices, passed_along(): lax.ppermute(value, axis, [(source, source + steps) for source in range(f...  544 us
    all_gather x1, waiting for transfers between devices, shards(): weights = lax.all_gather(qkv_weight[0], 'cp', axis=0, tiled=True)  63.3 us
    ppermute x27, starting transfers between devices, passed_along(): lax.ppermute(value, axis, [(source, source + steps) for source in range(f...  46.4 us
    select_n x9, other arithmetic, store(): return jnp.where(active, updated, collected)  25.8 us
    dot_general x2, matrix products, project(): jnp.dot(normed, weights, preferred_element_type=jnp.float32)  20.6 us
  transfers between devices with their start and end apart: 28, of which 28 were waited for; matrix products, arithmetic and copies ran while one was open for 4% of the time, Pallas kernels for 0%

commit v1 on v0

v1 whole, which is shorter than its diff:
```python
import functools
import math

import jax
import jax.numpy as jnp
from jax import lax
from jax.experimental import pallas as pl
from jax.experimental.pallas import tpu as pltpu
from jax.sharding import PartitionSpec as P

MESH = pl.DeviceIdType.MESH
KVHEADS = 4
HEAD = 128
GROUP = 4
WIDE = GROUP * HEAD
COLS = WIDE + 2 * HEAD
NX, NY = 4, 4
EPSILON = 1e-05
NEGATIVE = -1e30
BF, F32 = jnp.bfloat16, jnp.float32


def kernel(
    inp, gain, w, lens, shifts, blen, out,
    wv, xin, xn, new, keep, pass_on, kv, halo, qs, allow, live, sel_a, sel_b,
    s1s, s1r, s2s, s2r, s3s, s3r, s4s, s4r, ds, dr,
    hs, hr, zs, zr, as_, bs, br,
):
    z, r = lax.axis_index("section"), lax.axis_index("cp")
    last_z = lax.axis_size("section") - 1
    ranks = lax.axis_size("cp")
    c = r % 2
    x, y = (r // 2) % NX, r // (2 * NX)
    chunks, groups, rows = xin.shape[0], xin.shape[1], xin.shape[2]
    width = groups * WIDE
    back = halo.shape[3]

    def at(dx, dy):
        return (z, (((y + dy) % NY) * NX + (x + dx) % NX) * 2 + c)

    sibling = (z, r + 1 - 2 * c)
    right, left = (z, (r + 1) % ranks), (z, (r + ranks - 1) % ranks)
    above = ((z + 1) % (last_z + 1), r)
    below = ((z + last_z) % (last_z + 1), r)

    barrier = pltpu.get_barrier_semaphore()
    peers = [sibling, at(1, 0), at(3, 0), at(0, 1), at(0, 3), right, left, above, below]
    for peer in peers:
        pl.semaphore_signal(barrier, inc=1, device_id=peer, device_id_type=MESH)

    for g in range(groups):
        for f in range(2):
            part = pl.ds(32 * f, 32)
            wv[g, y, x, c, f, :, 0:WIDE] = w[0, part, g * WIDE : (g + 1) * WIDE]
            for k in range(2):
                first = width + (k * groups + g) * HEAD
                wv[g, y, x, c, f, :, WIDE + k * HEAD : WIDE + (k + 1) * HEAD] = w[
                    0, part, first : first + HEAD
                ]
    pl.semaphore_wait(barrier, len(peers))

    def send(src, dst, ss, rs, to):
        return pltpu.make_async_remote_copy(
            src_ref=src, dst_ref=dst, send_sem=ss, recv_sem=rs, device_id=to, device_id_type=MESH
        )

    def same(ref, ss, rs, to):
        return send(ref, ref, ss, rs, to)

    x1, x3, y1, y3 = (x + 1) % NX, (x + 3) % NX, (y + 1) % NY, (y + 3) % NY
    x2, y2 = (x + 2) % NX, (y + 2) % NY
    low, high = pl.ds(0, 16), pl.ds(16, 16)

    def step1(g):
        return [
            same(wv.at[g, y, x, c, 0], s1s.at[0, g, 0], s1r.at[0, g, 0], at(1, 0)),
            same(wv.at[g, y, x, c, 0], s1s.at[0, g, 1], s1r.at[0, g, 1], at(3, 0)),
            same(wv.at[g, y, x, c, 1], s1s.at[1, g, 0], s1r.at[1, g, 0], at(0, 1)),
            same(wv.at[g, y, x, c, 1], s1s.at[1, g, 1], s1r.at[1, g, 1], at(0, 3)),
        ]

    def step2(g):
        return [
            same(wv.at[g, y, x3, c, 0, low], s2s.at[0, g, 0], s2r.at[0, g, 0], at(1, 0)),
            same(wv.at[g, y, x1, c, 0, high], s2s.at[0, g, 1], s2r.at[0, g, 1], at(3, 0)),
            same(wv.at[g, y3, x, c, 1, low], s2s.at[1, g, 0], s2r.at[1, g, 0], at(0, 1)),
            same(wv.at[g, y1, x, c, 1, high], s2s.at[1, g, 1], s2r.at[1, g, 1], at(0, 3)),
        ]

    def step3(g):
        return [
            same(wv.at[g, y, :, c, 0], s3s.at[0, g, 0], s3r.at[0, g, 0], at(0, 1)),
            same(wv.at[g, y, :, c, 0], s3s.at[0, g, 1], s3r.at[0, g, 1], at(0, 3)),
            same(wv.at[g, :, x, c, 1], s3s.at[1, g, 0], s3r.at[1, g, 0], at(1, 0)),
            same(wv.at[g, :, x, c, 1], s3s.at[1, g, 1], s3r.at[1, g, 1], at(3, 0)),
        ]

    def step4(g):
        return [
            same(wv.at[g, y3, :, c, 0, low], s4s.at[0, g, 0], s4r.at[0, g, 0], at(0, 1)),
            same(wv.at[g, y1, :, c, 0, high], s4s.at[0, g, 1], s4r.at[0, g, 1], at(0, 3)),
            same(wv.at[g, :, x3, c, 1, low], s4s.at[1, g, 0], s4r.at[1, g, 0], at(1, 0)),
            same(wv.at[g, :, x1, c, 1, high], s4s.at[1, g, 1], s4r.at[1, g, 1], at(3, 0)),
        ]

    def share(g, which):
        row, col = ((y, x), (y3, x3), (y1, x1), (y2, x2))[which]
        return [
            same(wv.at[g, row, :, c, 0], ds.at[0, g, which], dr.at[0, g, which], sibling),
            same(wv.at[g, :, col, c, 1], ds.at[1, g, which], dr.at[1, g, which], sibling),
        ]

    def start(copies):
        for copy in copies:
            copy.start()

    def arrive(copies):
        for copy in copies:
            copy.wait_recv()

    def sent(copies):
        for copy in copies:
            copy.wait_send()

    @pl.loop(0, groups)
    def _(g):
        start(step1(g))

    spot = lax.broadcasted_iota(jnp.int32, (HEAD, HEAD), 0)
    until = lax.broadcasted_iota(jnp.int32, (HEAD, HEAD), 1)
    upto = jnp.where(spot <= until, 1.0, 0.0).astype(BF)
    length = lens[...].astype(F32)
    ends = jnp.dot(length.astype(BF), upto, preferred_element_type=F32)
    starts = ends - length
    moves = shifts[...].astype(F32)
    base = (r * rows).astype(F32)
    for q in range(chunks):
        begin, end, move = starts[q : q + 1], ends[q : q + 1], moves[q : q + 1]
        place = lax.broadcasted_iota(jnp.int32, (rows, HEAD), 0).astype(F32) + base
        before, after = begin <= place, end > place
        doc_start = jnp.max(jnp.where(before, begin, -1.0), axis=1, keepdims=True)
        doc_end = jnp.min(jnp.where(after, end, 1e9), axis=1, keepdims=True)
        shift = jnp.max(jnp.where(before & after, move, 0.0), axis=1, keepdims=True)
        edge = base + rows
        moved = (doc_start >= base) & (shift > 0.5) & (edge < float(rows) * ranks)
        to_next = jnp.where((doc_end > edge) | moved, 1.0, 0.0)
        alive = jnp.where(place < blen[q].astype(F32), 1.0, 0.0)
        live[q] = alive
        sel_a[q] = alive * (1.0 - to_next)
        sel_b[q] = alive * to_next
        span = (rows, back + rows)
        key = lax.broadcasted_iota(jnp.int32, span, 1).astype(F32) + (base - back)
        query = lax.broadcasted_iota(jnp.int32, span, 0).astype(F32) + base
        allow[q] = jnp.where((key >= doc_start) & (key <= query), 1.0, 0.0)

    @pl.when(r == 0)
    def _():
        halo[...] = jnp.zeros_like(halo)

    gains = gain[...]

    def norm(q):
        @pl.loop(0, rows // 16)
        def _(i):
            part = pl.ds(pl.multiple_of(i * 16, 16), 16)
            values = [xin[q, g, part].astype(F32) for g in range(groups)]
            total = sum(jnp.sum(v * v, axis=1, keepdims=True) for v in values)
            inverse = lax.rsqrt(total * (1.0 / width) + EPSILON)
            for g in range(groups):
                cols = slice(g * WIDE, (g + 1) * WIDE)
                xn[q, part, cols] = (values[g] * inverse * gains[:, cols]).astype(BF)

    def halo_copy(q, g):
        return send(kv.at[q, g], halo.at[q, g, 0], hs.at[q, g], hr.at[q, g], right)

    def relay(q, g):
        return send(new.at[q, g], xin.at[q, g], zs.at[q, g], zr.at[q, g], above)

    def columns(g):
        return pl.ds(pl.multiple_of(g * WIDE, WIDE), WIDE)

    def keep_copy(q, g):
        return pltpu.make_async_copy(
            keep.at[q, g], out.at[0, q, pl.ds(rows, rows), columns(g)], as_.at[q, g]
        )

    def pass_copy(q, g):
        return send(
            pass_on.at[q, g], out.at[0, q, pl.ds(0, rows), columns(g)],
            bs.at[q, g], br.at[q, g], right,
        )

    def weights(g, first, count):
        block = wv[g, :, :, :, :, :, first : first + count]
        return block.reshape(width, count)

    def project_kv(q, g):
        kv[q, g] = jnp.dot(
            xn[q], weights(g, WIDE, 2 * HEAD), preferred_element_type=F32
        ).astype(BF)

        @pl.when(r < ranks - 1)
        def _():
            halo_copy(q, g).start()

    def project_q(q, g):
        qs[q, g] = jnp.dot(
            xn[q], weights(g, 0, WIDE), preferred_element_type=F32
        ).astype(BF)

    def attend(q, g):
        @pl.when(r > 0)
        def _():
            halo_copy(q, g).wait_recv()

        keys = jnp.concatenate([halo[q, g, 0, :, 0:HEAD], kv[q, g, :, 0:HEAD]], axis=0)
        vals = jnp.concatenate([halo[q, g, 0, :, HEAD:], kv[q, g, :, HEAD:]], axis=0)
        for h in range(GROUP):
            cols = slice(h * HEAD, (h + 1) * HEAD)
            scores = lax.dot_general(
                qs[q, g, :, cols], keys, (((1,), (1,)), ((), ())), preferred_element_type=F32
            )
            scores = jnp.where(allow[q] > 0.5, scores * (1.0 / math.sqrt(HEAD)), NEGATIVE)
            highest = jnp.max(scores, axis=1, keepdims=True)
            weighted = jnp.exp(scores - highest)
            totals = jnp.sum(weighted, axis=1, keepdims=True)
            mixed = jnp.dot(weighted.astype(BF), vals, preferred_element_type=F32) / totals
            result = jnp.where(live[q] > 0.5, xin[q, g, :, cols].astype(F32) + mixed, 0.0)
            new[q, g, :, cols] = result.astype(BF)
            keep[q, g, :, cols] = jnp.where(sel_a[q] > 0.5, result, 0.0).astype(BF)
            pass_on[q, g, :, cols] = jnp.where(sel_b[q] > 0.5, result, 0.0).astype(BF)

        @pl.when(z < last_z)
        def _():
            relay(q, g).start()

        keep_copy(q, g).start()

        @pl.when(r < ranks - 1)
        def _():
            pass_copy(q, g).start()

    @pl.when(z == 0)
    def _():
        for q in range(chunks):
            for g in range(groups):
                xin[q, g] = inp[q, :, g * WIDE : (g + 1) * WIDE]

        @pl.loop(0, chunks)
        def _(q):
            norm(q)

    @pl.loop(0, groups)
    def _(g):
        arrive(step1(g))
        start(step2(g))

    def row_steps(g):
        arrive(step2(g))
        start(step3(g))
        start(share(g, 0))

    @pl.loop(0, 2)
    def _(g):
        row_steps(g)

    @pl.loop(0, groups + 1)
    def _(i):
        @pl.when(i < groups)
        def _():
            arrive(step3(i))
            start(step4(i))
            start(share(i, 1))
            start(share(i, 2))

            @pl.when(i + 2 < groups)
            def _():
                row_steps(i + 2)

        @pl.when(i > 0)
        def _():
            g = i - 1
            arrive(step4(g))
            start(share(g, 3))
            for which in range(4):
                arrive(share(g, which))

            @pl.when(z == 0)
            def _():
                @pl.loop(0, chunks)
                def _(q):
                    project_kv(q, g)

                @pl.loop(0, chunks)
                def _(q):
                    project_q(q, g)
                    attend(q, g)

    @pl.when(z > 0)
    def _():
        @pl.loop(0, chunks)
        def _(q):
            @pl.loop(0, groups)
            def _(g):
                relay(q, g).wait_recv()

            norm(q)

            @pl.loop(0, groups)
            def _(g):
                project_kv(q, g)

            @pl.loop(0, groups)
            def _(g):
                project_q(q, g)

            @pl.loop(0, groups)
            def _(g):
                attend(q, g)

    @pl.loop(0, groups)
    def _(g):
        sent(step1(g))
        sent(step2(g))
        sent(step3(g))
        sent(step4(g))
        for which in range(4):
            sent(share(g, which))

    @pl.loop(0, chunks)
    def _(q):
        @pl.loop(0, groups)
        def _(g):
            keep_copy(q, g).wait()

            @pl.when(z < last_z)
            def _():
                relay(q, g).wait_send()

            @pl.when(r < ranks - 1)
            def _():
                halo_copy(q, g).wait_send()
                pass_copy(q, g).wait_send()

            @pl.when(r > 0)
            def _():
                pass_copy(q, g).wait_recv()

            @pl.when(r == 0)
            def _():
                keep[q, g] = jnp.zeros_like(keep[q, g])
                blank = pltpu.make_async_copy(
                    keep.at[q, g], out.at[0, q, pl.ds(0, rows), columns(g)], as_.at[q, g]
                )
                blank.start()
                blank.wait()


def shards(inputs, norm_gain, qkv_weight, batch_lengths, doc_lengths, doc_shift):
    chunks, rows, width = inputs.shape
    groups = KVHEADS
    vmem = pl.BlockSpec(memory_space=pltpu.VMEM)
    smem = pl.BlockSpec(memory_space=pltpu.SMEM)
    dma = pltpu.SemaphoreType.DMA
    state = pltpu.VMEM((chunks, groups, rows, WIDE), BF)
    flags = pltpu.VMEM((chunks, rows, HEAD), F32)
    ring = dma((2, groups, 2))
    piece = dma((chunks, groups))
    return pl.pallas_call(
        kernel,
        out_shape=jax.ShapeDtypeStruct((1, chunks, 2 * rows, width), BF),
        in_specs=[vmem, vmem, vmem, vmem, vmem, smem],
        out_specs=pl.BlockSpec(memory_space=pl.ANY),
        scratch_shapes=[
            pltpu.VMEM((groups, NY, NX, 2, 2, 32, COLS), BF),
            state,
            pltpu.VMEM((chunks, rows, width), BF),
            state,
            state,
            state,
            pltpu.VMEM((chunks, groups, rows, 2 * HEAD), BF),
            pltpu.VMEM((chunks, groups, 1, rows, 2 * HEAD), BF),
            state,
            pltpu.VMEM((chunks, rows, 2 * rows), F32),
            flags,
            flags,
            flags,
            ring, ring, ring, ring, ring, ring, ring, ring,
            dma((2, groups, 4)), dma((2, groups, 4)),
            piece, piece, piece, piece, piece, piece, piece,
        ],
        compiler_params=pltpu.CompilerParams(
            collective_id=0, has_side_effects=True, vmem_limit_bytes=48 << 20
        ),
        name="relay",
    )(inputs, norm_gain, qkv_weight, doc_lengths, doc_shift, batch_lengths)


def solution(mesh):
    placed = (P(None, "cp", None), P("section", None), P("section", "cp", None), P(), P(), P())
    return jax.shard_map(
        shards,
        mesh=mesh,
        in_specs=placed,
        out_specs=P("section", None, "cp", None),
        check_vma=False,
    )
```

time: 808 us -> 235 us (0.29)
  waiting for transfers between devices: 608 us -> 0 us
  Pallas kernels: 0 us -> 228 us
  other arithmetic: 61.9 us -> 0 us
  starting transfers between devices: 46.4 us -> 0 us
  matrix products: 32.5 us -> 0 us
  local copies, waits for them, and re-layouts: 36.6 us -> 6.51 us
  between operations: 13.5 us -> 0.02 us
    ppermute x27 -> x0, waiting for transfers between devices: 544 us -> none  [passed_along(): lax.ppermute(value, axis, [(source, source + steps) for source in range(f...]
    pallas_call x0 -> x1, Pallas kernels: none -> 228 us  [shards(): pl.pallas_call(kernel, out_shape=jax.ShapeDtypeStruct((1, chunks, 2 * row...]
    all_gather x1 -> x0, waiting for transfers between devices: 63.3 us -> none  [shards(): weights = lax.all_gather(qkv_weight[0], 'cp', axis=0, tiled=True)]
    ppermute x27 -> x0, starting transfers between devices: 46.4 us -> none  [passed_along(): lax.ppermute(value, axis, [(source, source + steps) for source in range(f...]
    select_n x27 -> x0, other arithmetic: 39.8 us -> none  [the longest x9 25.8 us: store(): return jnp.where(active, updated, collected)]
    dot_general x6 -> x0, matrix products: 32.5 us -> none  [the longest x2 20.6 us: project(): jnp.dot(normed, weights, preferred_element_type=jnp.float32)]
    reshape x10 -> x0, local copies, waits for them, and re-layouts: 15.9 us -> none  [the longest x2 8.23 us: mix(): return mixture.reshape(queries.shape[0], -1)]
    slice x23 -> x0, local copies, waits for them, and re-layouts: 10.1 us -> none  [the longest x2 5.07 us: split_heads(): projected[:, :model_width]]
  transfers between devices with their start and end apart: 28 -> 0, of which waited for: 28 -> 0; matrix products, arithmetic and copies ran while one was open for 4% -> 0% of each run, Pallas kernels for 0% -> 0%
where the time goes in v1:
time: 235 us
  Pallas kernels  228 us (97%)
  local copies, waits for them, and re-layouts  6.51 us (3%)
    pallas_call x1, Pallas kernels, shards(): pl.pallas_call(kernel, out_shape=jax.ShapeDtypeStruct((1, chunks, 2 * row...  228 us
    unnamed x13, local copies, waits for them, and re-layouts  6.51 us

profile of v1, /device:TPU:240, one launch (start us, length us, event | category | flops | bytes accessed | tf_op | source)
XLA Modules:
  0.0 234.9 jit_solution(14846307599497989866)
XLA Ops:
  0.0 0.0 copy-start
  0.0 1.3 copy-done
  1.3 0.0 copy-start.1
  1.3 1.0 copy-done.1
  2.3 0.0 copy-start.2
  2.3 0.7 copy-done.2
  3.0 0.0 copy-start.3
  3.0 0.7 copy-done.3
  3.7 0.0 copy-start.4
  3.7 0.7 copy-done.4
  4.4 0.0 copy-start.5
  4.4 0.7 copy-done.5
  5.0 228.4 %relay.1 = bf16[1,2,320,2048]{3,2,1,0:T(8,128)(2,1)S(1)} custom-call(bf16[2,160,2048]{2,1,0:T(8,128)(2,1)S(1)} %copy-done, f32[1,2048]{1,0:T(1,128)S(1)} %copy-done.2, bf16[1,64,3072]{2,1,0:T(8,128)(2,1)S(1)} %copy-done.1, s32[2,128]{1,0:T(2,128)S(1)} %copy-done.3, s32[2,128]{1,0:T(2,128)S(1)} %copy-done.4, s32[2]{0:T(128)S(1)} %copy-done.5), custom_call_target="tpu_custom_call" | custom-call | tf_op jit(solution)/shard_map/relay/pallas_call | solution.py:369
  233.4 1.5 copy.8
Async XLA Ops:
  0.0 1.3 copy-start
  1.3 1.0 copy-start.1
  2.3 0.7 copy-start.2
  3.0 0.7 copy-start.3
  3.7 0.7 copy-start.4
  4.4 0.7 copy-start.5

commit v2 on v1

v2 whole, which is shorter than its diff:
```python
import functools
import math

import jax
import jax.numpy as jnp
from jax import lax
from jax.experimental import pallas as pl
from jax.experimental.pallas import tpu as pltpu
from jax.sharding import PartitionSpec as P

MESH = pl.DeviceIdType.MESH
KVHEADS = 4
HEAD = 128
GROUP = 4
WIDE = GROUP * HEAD
COLS = WIDE + 2 * HEAD
NX, NY = 4, 4
EPSILON = 1e-05
NEGATIVE = -1e30
BF, F32 = jnp.bfloat16, jnp.float32


def kernel(
    inp, gain_in, w, lens_in, shifts_in, blen_in, out,
    gain, lens, shifts, blen, fetched, wv, xin, xn, keep, pass_on, kv, halo, qs,
    allow, live, sel_a, sel_b, zero,
    s1s, s1r, s2s, s2r, s3s, s3r, s4s, s4r, ds, dr,
    hs, hr, zs, zr, as_, ar, bs, br, ws, wr, cleared,
):
    z, r = lax.axis_index("section"), lax.axis_index("cp")
    last_z = lax.axis_size("section") - 1
    ranks = lax.axis_size("cp")
    c = r % 2
    x, y = (r // 2) % NX, r // (2 * NX)
    chunks, groups, rows = xin.shape[0], xin.shape[1], xin.shape[2]
    width = groups * WIDE
    back = halo.shape[3]

    def at(dx, dy):
        return (z, (((y + dy) % NY) * NX + (x + dx) % NX) * 2 + c)

    sibling = (z, r + 1 - 2 * c)
    right, left = (r + 1) % ranks, (r + ranks - 1) % ranks

    odd = z % 2
    paired = odd * ((z + last_z - 2) // (last_z + 1))
    gives = (1 - odd) * ((z + last_z - 1) // (last_z + 1))
    works = 1 - gives
    blocks = groups * (works + paired)

    def up(k, rank):
        return ((z + k + last_z + 1) % (last_z + 1), rank)

    following = up(1 + (z + last_z) // (last_z + 1), r)

    barrier = pltpu.get_barrier_semaphore()
    peers = [sibling, at(1, 0), at(3, 0), at(0, 1), at(0, 3), (z, right), (z, left)]
    peers += [up(1, r), up(-1, r), up(2, r), up(-2, r), up(-1, right), up(1, left)]
    for peer in peers:
        pl.semaphore_signal(barrier, inc=1, device_id=peer, device_id_type=MESH)

    for g in range(groups):
        spans = (
            (0, g * WIDE, WIDE),
            (WIDE, width + g * HEAD, HEAD),
            (WIDE + HEAD, width + (groups + g) * HEAD, HEAD),
        )
        for f in range(2):
            for to, first, count in spans:
                pltpu.make_async_copy(
                    w.at[0, pl.ds(32 * f, 32), pl.ds(first, count)],
                    wv.at[g, y, x, c, f, :, pl.ds(to, count)],
                    fetched.at[0],
                ).start()
    small = [
        pltpu.make_async_copy(src, dst, fetched.at[1 + i])
        for i, (src, dst) in enumerate(
            ((lens_in, lens), (shifts_in, shifts), (blen_in, blen), (gain_in, gain.at[0]))
        )
    ]
    for copy in small:
        copy.start()

    @pl.when(z == 0)
    def _():
        for q in range(chunks):
            for g in range(groups):
                pltpu.make_async_copy(
                    inp.at[q, :, pl.ds(g * WIDE, WIDE)], xin.at[q, g], zr.at[q, g]
                ).start()

    mine = wv.at[pl.ds(0, groups), y, x, c]
    pltpu.make_async_copy(mine, mine, fetched.at[0]).wait()
    pl.semaphore_wait(barrier, len(peers))

    def send(src, dst, ss, rs, to):
        return pltpu.make_async_remote_copy(
            src_ref=src, dst_ref=dst, send_sem=ss, recv_sem=rs, device_id=to, device_id_type=MESH
        )

    def same(ref, ss, rs, to):
        return send(ref, ref, ss, rs, to)

    x1, x3, y1, y3 = (x + 1) % NX, (x + 3) % NX, (y + 1) % NY, (y + 3) % NY
    x2, y2 = (x + 2) % NX, (y + 2) % NY
    low, high = pl.ds(0, 16), pl.ds(16, 16)

    def step1(g):
        return [
            same(wv.at[g, y, x, c, 0], s1s.at[0, g, 0], s1r.at[0, g, 0], at(1, 0)),
            same(wv.at[g, y, x, c, 0], s1s.at[0, g, 1], s1r.at[0, g, 1], at(3, 0)),
            same(wv.at[g, y, x, c, 1], s1s.at[1, g, 0], s1r.at[1, g, 0], at(0, 1)),
            same(wv.at[g, y, x, c, 1], s1s.at[1, g, 1], s1r.at[1, g, 1], at(0, 3)),
        ]

    def step2(g):
        return [
            same(wv.at[g, y, x3, c, 0, low], s2s.at[0, g, 0], s2r.at[0, g, 0], at(1, 0)),
            same(wv.at[g, y, x1, c, 0, high], s2s.at[0, g, 1], s2r.at[0, g, 1], at(3, 0)),
            same(wv.at[g, y3, x, c, 1, low], s2s.at[1, g, 0], s2r.at[1, g, 0], at(0, 1)),
            same(wv.at[g, y1, x, c, 1, high], s2s.at[1, g, 1], s2r.at[1, g, 1], at(0, 3)),
        ]

    def step3(g):
        return [
            same(wv.at[g, y, :, c, 0], s3s.at[0, g, 0], s3r.at[0, g, 0], at(0, 1)),
            same(wv.at[g, y, :, c, 0], s3s.at[0, g, 1], s3r.at[0, g, 1], at(0, 3)),
            same(wv.at[g, :, x, c, 1], s3s.at[1, g, 0], s3r.at[1, g, 0], at(1, 0)),
            same(wv.at[g, :, x, c, 1], s3s.at[1, g, 1], s3r.at[1, g, 1], at(3, 0)),
        ]

    def step4(g):
        return [
            same(wv.at[g, y3, :, c, 0, low], s4s.at[0, g, 0], s4r.at[0, g, 0], at(0, 1)),
            same(wv.at[g, y1, :, c, 0, high], s4s.at[0, g, 1], s4r.at[0, g, 1], at(0, 3)),
            same(wv.at[g, :, x3, c, 1, low], s4s.at[1, g, 0], s4r.at[1, g, 0], at(1, 0)),
            same(wv.at[g, :, x1, c, 1, high], s4s.at[1, g, 1], s4r.at[1, g, 1], at(3, 0)),
        ]

    def share(g, which):
        row, col = ((y, x), (y3, x3), (y1, x1), (y2, x2))[which]
        return [
            same(wv.at[g, row, :, c, 0], ds.at[0, g, which], dr.at[0, g, which], sibling),
            same(wv.at[g, :, col, c, 1], ds.at[1, g, which], dr.at[1, g, which], sibling),
        ]

    def start(copies):
        for copy in copies:
            copy.start()

    def arrive(copies):
        for copy in copies:
            copy.wait_recv()

    def sent(copies):
        for copy in copies:
            copy.wait_send()

    @pl.loop(0, groups * works)
    def _(g):
        start(step1(g))

    handed = [
        send(mine, wv.at[pl.ds(groups, groups), y, x, c], ws.at[0], wr.at[0], up(1, r)),
        send(gain.at[0], gain.at[1], ws.at[1], wr.at[1], up(1, r)),
    ]

    @pl.when(gives == 1)
    def _():
        handed[0].start()

    for copy in small:
        copy.wait()

    @pl.when(gives == 1)
    def _():
        handed[1].start()

    spot = lax.broadcasted_iota(jnp.int32, (HEAD, HEAD), 0)
    until = lax.broadcasted_iota(jnp.int32, (HEAD, HEAD), 1)
    upto = jnp.where(spot <= until, 1.0, 0.0).astype(BF)
    length = lens[...].astype(F32)
    ends = jnp.dot(length.astype(BF), upto, preferred_element_type=F32)
    starts = ends - length
    moves = shifts[...].astype(F32)
    base = (r * rows).astype(F32)
    for q in range(chunks):
        begin, end, move = starts[q : q + 1], ends[q : q + 1], moves[q : q + 1]
        place = lax.broadcasted_iota(jnp.int32, (rows, HEAD), 0).astype(F32) + base
        before, after = begin <= place, end > place
        doc_start = jnp.max(jnp.where(before, begin, -1.0), axis=1, keepdims=True)
        doc_end = jnp.min(jnp.where(after, end, 1e9), axis=1, keepdims=True)
        shift = jnp.max(jnp.where(before & after, move, 0.0), axis=1, keepdims=True)
        edge = base + rows
        moved = (doc_start >= base) & (shift > 0.5) & (edge < float(rows) * ranks)
        to_next = jnp.where((doc_end > edge) | moved, 1.0, 0.0)
        alive = jnp.where(place < blen[q].astype(F32), 1.0, 0.0)
        live[q] = alive
        sel_a[q] = alive * (1.0 - to_next)
        sel_b[q] = alive * to_next
        span = (rows, back + rows)
        key = lax.broadcasted_iota(jnp.int32, span, 1).astype(F32) + (base - back)
        query = lax.broadcasted_iota(jnp.int32, span, 0).astype(F32) + base
        allow[q] = jnp.where((key >= doc_start) & (key <= query), 1.0, 0.0)

    @pl.when(r == 0)
    def _():
        halo[...] = jnp.zeros_like(halo)

    def columns(g):
        return pl.ds(pl.multiple_of(g * WIDE, WIDE), WIDE)

    def blank(q, g):
        return pltpu.make_async_copy(
            zero, out.at[0, q, pl.ds(0, rows), columns(g)], cleared.at[0]
        )

    @pl.when(r == 0)
    def _():
        zero[...] = jnp.zeros_like(zero)

        @pl.loop(0, chunks)
        def _(q):
            @pl.loop(0, groups)
            def _(g):
                blank(q, g).start()

    def norm(s, q):
        gains = gain[s]


        @pl.loop(0, rows // 32)
        def _(i):
            part = pl.ds(pl.multiple_of(i * 32, 32), 32)
            values = [xin[q, g, part].astype(F32) for g in range(groups)]
            total = sum(jnp.sum(v * v, axis=1, keepdims=True) for v in values)
            inverse = lax.rsqrt(total * (1.0 / width) + EPSILON)
            for g in range(groups):
                cols = slice(g * WIDE, (g + 1) * WIDE)
                xn[part, cols] = (values[g] * inverse * gains[:, cols]).astype(BF)

    def halo_copy(t, g):
        return send(kv.at[t, g], halo.at[t, g, 0], hs.at[t, g], hr.at[t, g], (z, right))

    def relay(q, g):
        return send(xin.at[q, g], xin.at[q, g], zs.at[q, g], zr.at[q, g], following)

    def keep_local(q, g):
        return pltpu.make_async_copy(
            keep.at[q, g], out.at[0, q, pl.ds(rows, rows), columns(g)], ar.at[q, g]
        )

    def keep_below(q, g):
        return send(
            keep.at[chunks + q, g], out.at[0, q, pl.ds(rows, rows), columns(g)],
            as_.at[q, g], ar.at[q, g], up(-1, r),
        )

    def pass_copy(s, q, g):
        return send(
            pass_on.at[s * chunks + q, g], out.at[0, q, pl.ds(0, rows), columns(g)],
            bs.at[s * chunks + q, g], br.at[q, g], up(-s, right),
        )

    def weights(s, g, first, count):
        block = wv[s * groups + g, :, :, :, :, :, first : first + count]
        return block.reshape(width, count)

    def project_kv(s, q, g):
        t = s * chunks + q
        kv[t, g] = jnp.dot(
            xn[...], weights(s, g, WIDE, 2 * HEAD), preferred_element_type=F32
        ).astype(BF)

        @pl.when(r < ranks - 1)
        def _():
            halo_copy(t, g).start()

    def project_q(s, g):
        qs[g] = jnp.dot(xn[...], weights(s, g, 0, WIDE), preferred_element_type=F32).astype(BF)

    def attend(s, q, g):
        t = s * chunks + q

        @pl.when(r > 0)
        def _():
            halo_copy(t, g).wait_recv()

        keys = jnp.concatenate([halo[t, g, 0, :, 0:HEAD], kv[t, g, :, 0:HEAD]], axis=0)
        vals = jnp.concatenate([halo[t, g, 0, :, HEAD:], kv[t, g, :, HEAD:]], axis=0)
        seen, alive = allow[q] > 0.5, live[q] > 0.5
        heads = [slice(h * HEAD, (h + 1) * HEAD) for h in range(GROUP)]
        scores = [
            lax.dot_general(
                qs[g, :, cols], keys, (((1,), (1,)), ((), ())), preferred_element_type=F32
            )
            for cols in heads
        ]
        scores = [jnp.where(seen, s * (1.0 / math.sqrt(HEAD)), NEGATIVE) for s in scores]
        highest = [jnp.max(s, axis=1, keepdims=True) for s in scores]
        weighted = [jnp.exp(s - m) for s, m in zip(scores, highest)]
        totals = [jnp.sum(e, axis=1, keepdims=True) for e in weighted]
        mixed = [jnp.dot(e.astype(BF), vals, preferred_element_type=F32) for e in weighted]
        for cols, mix, total in zip(heads, mixed, totals):
            result = jnp.where(alive, xin[q, g, :, cols].astype(F32) + mix / total, 0.0)
            xin[q, g, :, cols] = result.astype(BF)

        @pl.when((s == 0) & (z < last_z))
        def _():
            relay(q, g).start()

        for cols in heads:
            result = xin[q, g, :, cols]
            keep[t, g, :, cols] = jnp.where(sel_a[q] > 0.5, result, 0.0).astype(BF)
            pass_on[t, g, :, cols] = jnp.where(sel_b[q] > 0.5, result, 0.0).astype(BF)

        @pl.when(s == 0)
        def _():
            keep_local(q, g).start()

        @pl.when(s == 1)
        def _():
            keep_below(q, g).start()

        @pl.when(r < ranks - 1)
        def _():
            pass_copy(s, q, g).start()

    def take(q):
        @pl.loop(0, groups)
        def _(g):
            relay(q, g).wait_recv()

    @pl.loop(0, groups * works)
    def _(g):
        arrive(step1(g))
        start(step2(g))

    @pl.when(paired == 1)
    def _():
        handed[0].wait_recv()

        @pl.loop(groups, 2 * groups)
        def _(g):
            start(step1(g))

    def row_steps(g):
        arrive(step2(g))
        start(step3(g))
        start(share(g, 0))

    @pl.loop(0, 2 * works)
    def _(g):
        row_steps(g)

    @pl.loop(0, blocks + works)
    def _(i):
        @pl.when(i < blocks)
        def _():
            arrive(step3(i))
            start(step4(i))
            start(share(i, 1))
            start(share(i, 2))

            @pl.when(i + 2 < blocks)
            def _():
                row_steps(i + 2)

            @pl.when(i + groups < blocks)
            def _():
                arrive(step1(i + groups))
                start(step2(i + groups))

        @pl.when(i > 0)
        def _():
            g = i - 1
            arrive(step4(g))
            start(share(g, 3))
            for which in range(4):
                arrive(share(g, which))

            @pl.when((z == 0) & (g == 0))
            def _():
                take(0)
                norm(0, 0)

            @pl.when(z == 0)
            def _():
                project_kv(0, 0, g)
                project_q(0, g)
                attend(0, 0, g)

    @pl.when(paired == 1)
    def _():
        handed[1].wait_recv()

    @pl.loop(1 - (z + last_z) // (last_z + 1), chunks * works)
    def _(q):
        take(q)

        @pl.loop(0, 1 + paired)
        def _(k):
            s = paired - k
            norm(s, q)
            for g in range(groups):
                project_kv(s, q, g)
            for g in range(groups):
                project_q(s, g)

            @pl.loop(0, groups)
            def _(g):
                attend(s, q, g)

    @pl.loop(0, blocks)
    def _(g):
        sent(step1(g))
        sent(step2(g))
        sent(step3(g))
        sent(step4(g))
        for which in range(4):
            sent(share(g, which))

    @pl.when(gives == 1)
    def _():
        sent(handed)

    @pl.loop(0, chunks)
    def _(q):
        @pl.loop(0, groups)
        def _(g):
            @pl.loop(0, works + paired)
            def _(s):
                @pl.when(r < ranks - 1)
                def _():
                    halo_copy(s * chunks + q, g).wait_send()
                    pass_copy(s, q, g).wait_send()

            @pl.when(paired == 1)
            def _():
                keep_below(q, g).wait_send()

            @pl.when((works == 1) & (z < last_z))
            def _():
                relay(q, g).wait_send()

            keep_below(q, g).wait_recv()

            @pl.when(r > 0)
            def _():
                pass_copy(0, q, g).wait_recv()

    @pl.when(r == 0)
    def _():
        first = out.at[0, :, pl.ds(0, rows)]
        pltpu.make_async_copy(first, first, cleared.at[0]).wait()


def shards(inputs, norm_gain, qkv_weight, batch_lengths, doc_lengths, doc_shift):
    chunks, rows, width = inputs.shape
    groups = KVHEADS
    there = pl.BlockSpec(memory_space=pl.ANY)
    dma = pltpu.SemaphoreType.DMA
    state = pltpu.VMEM((chunks, groups, rows, WIDE), BF)
    flags = pltpu.VMEM((chunks, rows, HEAD), F32)
    both = pltpu.VMEM((2 * chunks, groups, rows, WIDE), BF)
    ring = dma((2, 2 * groups, 2))
    piece, tasks = dma((chunks, groups)), dma((2 * chunks, groups))
    return pl.pallas_call(
        kernel,
        out_shape=jax.ShapeDtypeStruct((1, chunks, 2 * rows, width), BF),
        in_specs=[there] * 6,
        out_specs=there,
        scratch_shapes=[
            pltpu.VMEM((2,) + norm_gain.shape, F32),
            pltpu.VMEM(doc_lengths.shape, jnp.int32),
            pltpu.VMEM(doc_shift.shape, jnp.int32),
            pltpu.SMEM(batch_lengths.shape, jnp.int32),
            dma((5,)),
            pltpu.VMEM((2 * groups, NY, NX, 2, 2, 32, COLS), BF),
            state,
            pltpu.VMEM((rows, width), BF),
            both,
            both,
            pltpu.VMEM((2 * chunks, groups, rows, 2 * HEAD), BF),
            pltpu.VMEM((2 * chunks, groups, 1, rows, 2 * HEAD), BF),
            pltpu.VMEM((groups, rows, WIDE), BF),
            pltpu.VMEM((chunks, rows, 2 * rows), F32),
            flags,
            flags,
            flags,
            pltpu.VMEM((rows, WIDE), BF),
            ring, ring, ring, ring, ring, ring, ring, ring,
            dma((2, 2 * groups, 4)), dma((2, 2 * groups, 4)),
            tasks, tasks, piece, piece, piece, piece, tasks, piece,
            dma((2,)), dma((2,)), dma((1,)),
        ],
        compiler_params=pltpu.CompilerParams(
            collective_id=0, has_side_effects=True, vmem_limit_bytes=48 << 20
        ),
        name="relay",
    )(inputs, norm_gain, qkv_weight, doc_lengths, doc_shift, batch_lengths)


def solution(mesh):
    placed = (P(None, "cp", None), P("section", None), P("section", "cp", None), P(), P(), P())
    return jax.shard_map(
        shards,
        mesh=mesh,
        in_specs=placed,
        out_specs=P("section", None, "cp", None),
        check_vma=False,
    )
```

time: 235 us -> 207 us (0.88); the launches traced: 235 us -> 204 us
  Pallas kernels: 228 us -> 198 us
    pallas_call x1, Pallas kernels: 228 us -> 198 us  [shards(): pl.pallas_call(kernel, out_shape=jax.ShapeDtypeStruct((1, chunks, 2 * row...]
where the time goes in v2:
time: 207 us; the launch traced here: 204 us
  Pallas kernels  198 us (96%)
  local copies, waits for them, and re-layouts  6.51 us (3%)
    pallas_call x1, Pallas kernels, shards(): pl.pallas_call(kernel, out_shape=jax.ShapeDtypeStruct((1, chunks, 2 * row...  198 us
    unnamed x13, local copies, waits for them, and re-layouts  6.51 us

profile of v2, /device:TPU:240, one launch (start us, length us, event | category | flops | bytes accessed | tf_op | source)
XLA Modules:
  0.0 204.3 jit_solution(3938501464288277085)
XLA Ops:
  0.0 0.0 copy-start
  0.0 1.3 copy-done
  1.3 0.0 copy-start.1
  1.3 1.0 copy-done.1
  2.3 0.0 copy-start.2
  2.3 0.7 copy-done.2
  3.0 0.0 copy-start.3
  3.0 0.7 copy-done.3
  3.7 0.0 copy-start.4
  3.7 0.7 copy-done.4
  4.4 0.0 copy-start.5
  4.4 0.7 copy-done.5
  5.0 197.8 %relay.1 = bf16[1,2,320,2048]{3,2,1,0:T(8,128)(2,1)S(1)} custom-call(bf16[2,160,2048]{2,1,0:T(8,128)(2,1)S(1)} %copy-done, f32[1,2048]{1,0:T(1,128)S(1)} %copy-done.2, bf16[1,64,3072]{2,1,0:T(8,128)(2,1)S(1)} %copy-done.1, s32[2,128]{1,0:T(2,128)S(1)} %copy-done.3, s32[2,128]{1,0:T(2,128)S(1)} %copy-done.4, s32[2]{0:T(128)S(1)} %copy-done.5), custom_call_target="tpu_custom_call" | custom-call | tf_op jit(solution)/shard_map/relay/pallas_call | solution.py:468
  202.8 1.5 copy.8
Async XLA Ops:
  0.0 1.3 copy-start
  1.3 1.0 copy-start.1
  2.3 0.7 copy-start.2
  3.0 0.7 copy-start.3
  3.7 0.7 copy-start.4
  4.4 0.7 copy-start.5

commit v3 on v2

--- a/solution.py
+++ b/solution.py
@@ -22,7 +22,7 @@
 
 def kernel(
     inp, gain_in, w, lens_in, shifts_in, blen_in, out,
-    gain, lens, shifts, blen, fetched, wv, xin, xn, keep, pass_on, kv, halo, qs,
+    gain, lens, shifts, blen, fetched, wv, xin, xn, raw, keep, pass_on, kv, halo, qs,
     allow, live, sel_a, sel_b, zero,
     s1s, s1r, s2s, s2r, s3s, s3r, s4s, s4r, ds, dr,
     hs, hr, zs, zr, as_, ar, bs, br, ws, wr, cleared,
@@ -55,7 +55,7 @@
 
     barrier = pltpu.get_barrier_semaphore()
     peers = [sibling, at(1, 0), at(3, 0), at(0, 1), at(0, 3), (z, right), (z, left)]
-    peers += [up(1, r), up(-1, r), up(2, r), up(-2, r), up(-1, right), up(1, left)]
+    peers += [up(1, r), up(-1, r), up(2, r), up(-2, r)]
     for peer in peers:
         pl.semaphore_signal(barrier, inc=1, device_id=peer, device_id_type=MESH)
 
@@ -245,22 +245,31 @@
     def relay(q, g):
         return send(xin.at[q, g], xin.at[q, g], zs.at[q, g], zr.at[q, g], following)
 
-    def keep_local(q, g):
+    def hand_back(q, g):
+        return send(raw.at[q, g], xin.at[q, g], as_.at[q, g], zr.at[q, g], up(-1, r))
+
+    def keep_copy(q, g):
         return pltpu.make_async_copy(
             keep.at[q, g], out.at[0, q, pl.ds(rows, rows), columns(g)], ar.at[q, g]
         )
 
-    def keep_below(q, g):
+    def pass_copy(q, g):
         return send(
-            keep.at[chunks + q, g], out.at[0, q, pl.ds(rows, rows), columns(g)],
-            as_.at[q, g], ar.at[q, g], up(-1, r),
+            pass_on.at[q, g], out.at[0, q, pl.ds(0, rows), columns(g)],
+            bs.at[q, g], br.at[q, g], (z, right),
         )
 
-    def pass_copy(s, q, g):
-        return send(
-            pass_on.at[s * chunks + q, g], out.at[0, q, pl.ds(0, rows), columns(g)],
-            bs.at[s * chunks + q, g], br.at[q, g], up(-s, right),
-        )
+    def deliver(q, g):
+        for h in range(GROUP):
+            cols = slice(h * HEAD, (h + 1) * HEAD)
+            result = xin[q, g, :, cols]
+            keep[q, g, :, cols] = jnp.where(sel_a[q] > 0.5, result, 0.0).astype(BF)
+            pass_on[q, g, :, cols] = jnp.where(sel_b[q] > 0.5, result, 0.0).astype(BF)
+        keep_copy(q, g).start()
+
+        @pl.when(r < ranks - 1)
+        def _():
+            pass_copy(q, g).start()
 
     def weights(s, g, first, count):
         block = wv[s * groups + g, :, :, :, :, :, first : first + count]
@@ -309,22 +318,14 @@
         def _():
             relay(q, g).start()
 
-        for cols in heads:
-            result = xin[q, g, :, cols]
-            keep[t, g, :, cols] = jnp.where(sel_a[q] > 0.5, result, 0.0).astype(BF)
-            pass_on[t, g, :, cols] = jnp.where(sel_b[q] > 0.5, result, 0.0).astype(BF)
-
-        @pl.when(s == 0)
-        def _():
-            keep_local(q, g).start()
-
         @pl.when(s == 1)
         def _():
-            keep_below(q, g).start()
-
-        @pl.when(r < ranks - 1)
-        def _():
-            pass_copy(s, q, g).start()
+            raw[q, g] = xin[q, g]
+            hand_back(q, g).start()
+
+        @pl.when((s == 0) & (z == last_z))
+        def _():
+            deliver(q, g)
 
     def take(q):
         @pl.loop(0, groups)
@@ -411,6 +412,18 @@
             def _(g):
                 attend(s, q, g)
 
+    @pl.when(z < last_z)
+    def _():
+        @pl.loop(0, chunks)
+        def _(q):
+            @pl.loop(0, groups)
+            def _(g):
+                @pl.when(gives == 1)
+                def _():
+                    hand_back(q, g).wait_recv()
+
+                deliver(q, g)
+
     @pl.loop(0, blocks)
     def _(g):
         sent(step1(g))
@@ -428,26 +441,27 @@
     def _(q):
         @pl.loop(0, groups)
         def _(g):
-            @pl.loop(0, works + paired)
-            def _(s):
-                @pl.when(r < ranks - 1)
-                def _():
+            @pl.when(r < ranks - 1)
+            def _():
+                @pl.loop(0, works + paired)
+                def _(s):
                     halo_copy(s * chunks + q, g).wait_send()
-                    pass_copy(s, q, g).wait_send()
+
+                pass_copy(q, g).wait_send()
 
             @pl.when(paired == 1)
             def _():
-                keep_below(q, g).wait_send()
+                hand_back(q, g).wait_send()
 
             @pl.when((works == 1) & (z < last_z))
             def _():
                 relay(q, g).wait_send()
 
-            keep_below(q, g).wait_recv()
+            keep_copy(q, g).wait()
 
             @pl.when(r > 0)
             def _():
-                pass_copy(0, q, g).wait_recv()
+                pass_copy(q, g).wait_recv()
 
     @pl.when(r == 0)
     def _():
@@ -462,7 +476,6 @@
     dma = pltpu.SemaphoreType.DMA
     state = pltpu.VMEM((chunks, groups, rows, WIDE), BF)
     flags = pltpu.VMEM((chunks, rows, HEAD), F32)
-    both = pltpu.VMEM((2 * chunks, groups, rows, WIDE), BF)
     ring = dma((2, 2 * groups, 2))
     piece, tasks = dma((chunks, groups)), dma((2 * chunks, groups))
     return pl.pallas_call(
@@ -479,8 +492,9 @@
             pltpu.VMEM((2 * groups, NY, NX, 2, 2, 32, COLS), BF),
             state,
             pltpu.VMEM((rows, width), BF),
-            both,
-            both,
+            state,
+            state,
+            state,
             pltpu.VMEM((2 * chunks, groups, rows, 2 * HEAD), BF),
             pltpu.VMEM((2 * chunks, groups, 1, rows, 2 * HEAD), BF),
             pltpu.VMEM((groups, rows, WIDE), BF),
@@ -491,7 +505,7 @@
             pltpu.VMEM((rows, WIDE), BF),
             ring, ring, ring, ring, ring, ring, ring, ring,
             dma((2, 2 * groups, 4)), dma((2, 2 * groups, 4)),
-            tasks, tasks, piece, piece, piece, piece, tasks, piece,
+            tasks, tasks, piece, piece, piece, piece, piece, piece,
             dma((2,)), dma((2,)), dma((1,)),
         ],
         compiler_params=pltpu.CompilerParams(

time: 207 us -> 178 us (0.86)
  Pallas kernels: 198 us -> 171 us
    pallas_call x1, Pallas kernels: 198 us -> 171 us  [shards(): pl.pallas_call(kernel, out_shape=jax.ShapeDtypeStruct((1, chunks, 2 * row...]
where the time goes in v3:
time: 178 us; the launch traced here: 177 us
  Pallas kernels  171 us (96%)
  local copies, waits for them, and re-layouts  6.51 us (4%)
    pallas_call x1, Pallas kernels, shards(): pl.pallas_call(kernel, out_shape=jax.ShapeDtypeStruct((1, chunks, 2 * row...  171 us
    unnamed x13, local copies, waits for them, and re-layouts  6.51 us

profile of v3, /device:TPU:240, one launch (start us, length us, event | category | flops | bytes accessed | tf_op | source)
XLA Modules:
  0.0 177.1 jit_solution(13869807863714047338)
XLA Ops:
  0.0 0.0 copy-start
  0.0 1.3 copy-done
  1.3 0.0 copy-start.1
  1.3 1.0 copy-done.1
  2.3 0.0 copy-start.2
  2.3 0.7 copy-done.2
  3.0 0.0 copy-start.3
  3.0 0.7 copy-done.3
  3.7 0.0 copy-start.4
  3.7 0.7 copy-done.4
  4.4 0.0 copy-start.5
  4.4 0.7 copy-done.5
  5.0 170.6 %relay.1 = bf16[1,2,320,2048]{3,2,1,0:T(8,128)(2,1)S(1)} custom-call(bf16[2,160,2048]{2,1,0:T(8,128)(2,1)S(1)} %copy-done, f32[1,2048]{1,0:T(1,128)S(1)} %copy-done.2, bf16[1,64,3072]{2,1,0:T(8,128)(2,1)S(1)} %copy-done.1, s32[2,128]{1,0:T(2,128)S(1)} %copy-done.3, s32[2,128]{1,0:T(2,128)S(1)} %copy-done.4, s32[2]{0:T(128)S(1)} %copy-done.5), custom_call_target="tpu_custom_call" | custom-call | tf_op jit(solution)/shard_map/relay/pallas_call | solution.py:481
  175.6 1.5 copy.8
Async XLA Ops:
  0.0 1.3 copy-start
  1.3 1.0 copy-start.1
  2.3 0.7 copy-start.2
  3.0 0.7 copy-start.3
  3.7 0.7 copy-start.4
  4.4 0.7 copy-start.5

commit v4 on v3

--- a/solution.py
+++ b/solution.py
@@ -18,6 +18,7 @@
 EPSILON = 1e-05
 NEGATIVE = -1e30
 BF, F32 = jnp.bfloat16, jnp.float32
+STEP = 1
 
 
 def kernel(
@@ -34,7 +35,7 @@
     x, y = (r // 2) % NX, r // (2 * NX)
     chunks, groups, rows = xin.shape[0], xin.shape[1], xin.shape[2]
     width = groups * WIDE
-    back = halo.shape[3]
+    back, half = rows, rows // 2
 
     def at(dx, dy):
         return (z, (((y + dy) % NY) * NX + (x + dx) % NX) * 2 + c)
@@ -46,7 +47,7 @@
     paired = odd * ((z + last_z - 2) // (last_z + 1))
     gives = (1 - odd) * ((z + last_z - 1) // (last_z + 1))
     works = 1 - gives
-    blocks = groups * (works + paired)
+    blocks = groups * works + (groups - 1) * paired + gives
 
     def up(k, rank):
         return ((z + k + last_z + 1) % (last_z + 1), rank)
@@ -58,6 +59,9 @@
     peers += [up(1, r), up(-1, r), up(2, r), up(-2, r)]
     for peer in peers:
         pl.semaphore_signal(barrier, inc=1, device_id=peer, device_id_type=MESH)
+
+    def slot(s, g):
+        return s * groups + (g + s * (groups - 1)) % groups
 
     for g in range(groups):
         spans = (
@@ -69,11 +73,11 @@
             for to, first, count in spans:
                 pltpu.make_async_copy(
                     w.at[0, pl.ds(32 * f, 32), pl.ds(first, count)],
-                    wv.at[g, y, x, c, f, :, pl.ds(to, count)],
-                    fetched.at[0],
+                    wv.at[slot(0, g), y, x, c, f, :, pl.ds(to, count)],
+                    fetched.at[g],
                 ).start()
     small = [
-        pltpu.make_async_copy(src, dst, fetched.at[1 + i])
+        pltpu.make_async_copy(src, dst, fetched.at[groups + i])
         for i, (src, dst) in enumerate(
             ((lens_in, lens), (shifts_in, shifts), (blen_in, blen), (gain_in, gain.at[0]))
         )
@@ -89,8 +93,10 @@
                     inp.at[q, :, pl.ds(g * WIDE, WIDE)], xin.at[q, g], zr.at[q, g]
                 ).start()
 
-    mine = wv.at[pl.ds(0, groups), y, x, c]
-    pltpu.make_async_copy(mine, mine, fetched.at[0]).wait()
+    mine = wv.at[pl.ds(1, groups - 1), y, x, c]
+    for g in range(groups):
+        block = wv.at[slot(0, g), y, x, c]
+        pltpu.make_async_copy(block, block, fetched.at[g]).wait()
     pl.semaphore_wait(barrier, len(peers))
 
     def send(src, dst, ss, rs, to):
@@ -156,12 +162,14 @@
         for copy in copies:
             copy.wait_send()
 
-    @pl.loop(0, groups * works)
+    first = works * groups + gives
+
+    @pl.loop(0, first)
     def _(g):
         start(step1(g))
 
     handed = [
-        send(mine, wv.at[pl.ds(groups, groups), y, x, c], ws.at[0], wr.at[0], up(1, r)),
+        send(mine, wv.at[pl.ds(groups, groups - 1), y, x, c], ws.at[0], wr.at[0], up(1, r)),
         send(gain.at[0], gain.at[1], ws.at[1], wr.at[1], up(1, r)),
     ]
 
@@ -198,10 +206,13 @@
         live[q] = alive
         sel_a[q] = alive * (1.0 - to_next)
         sel_b[q] = alive * to_next
-        span = (rows, back + rows)
-        key = lax.broadcasted_iota(jnp.int32, span, 1).astype(F32) + (base - back)
-        query = lax.broadcasted_iota(jnp.int32, span, 0).astype(F32) + base
-        allow[q] = jnp.where((key >= doc_start) & (key <= query), 1.0, 0.0)
+        for i in range(2):
+            part = slice(i * half, (i + 1) * half)
+            span = (half, back + half)
+            query = lax.broadcasted_iota(jnp.int32, span, 0).astype(F32) + (base + i * half)
+            key = lax.broadcasted_iota(jnp.int32, span, 1).astype(F32) + (base + i * half - back)
+            seen = (key >= doc_start[part]) & (key <= query)
+            allow[q, i] = jnp.where(seen, 1.0, 0.0)
 
     @pl.when(r == 0)
     def _():
@@ -229,9 +240,9 @@
         gains = gain[s]
 
 
-        @pl.loop(0, rows // 32)
+        @pl.loop(0, rows // half)
         def _(i):
-            part = pl.ds(pl.multiple_of(i * 32, 32), 32)
+            part = pl.ds(pl.multiple_of(i * half, half), half)
             values = [xin[q, g, part].astype(F32) for g in range(groups)]
             total = sum(jnp.sum(v * v, axis=1, keepdims=True) for v in values)
             inverse = lax.rsqrt(total * (1.0 / width) + EPSILON)
@@ -272,7 +283,7 @@
             pass_copy(q, g).start()
 
     def weights(s, g, first, count):
-        block = wv[s * groups + g, :, :, :, :, :, first : first + count]
+        block = wv[slot(s, g), :, :, :, :, :, first : first + count]
         return block.reshape(width, count)
 
     def project_kv(s, q, g):
@@ -288,32 +299,56 @@
     def project_q(s, g):
         qs[g] = jnp.dot(xn[...], weights(s, g, 0, WIDE), preferred_element_type=F32).astype(BF)
 
-    def attend(s, q, g):
+    heads = [slice(h * HEAD, (h + 1) * HEAD) for h in range(GROUP)]
+    parts = [slice(i * half, (i + 1) * half) for i in range(2)]
+
+    def attend(s, q, some):
         t = s * chunks + q
-
-        @pl.when(r > 0)
-        def _():
-            halo_copy(t, g).wait_recv()
-
-        keys = jnp.concatenate([halo[t, g, 0, :, 0:HEAD], kv[t, g, :, 0:HEAD]], axis=0)
-        vals = jnp.concatenate([halo[t, g, 0, :, HEAD:], kv[t, g, :, HEAD:]], axis=0)
-        seen, alive = allow[q] > 0.5, live[q] > 0.5
-        heads = [slice(h * HEAD, (h + 1) * HEAD) for h in range(GROUP)]
+        for g in some:
+
+            @pl.when(r > 0)
+            def _():
+                halo_copy(t, g).wait_recv()
+
+        def seen_rows(g, i, cols):
+            earlier, own = halo[t, g, 0, i * half :, cols], kv[t, g, : (i + 1) * half, cols]
+            return jnp.concatenate([earlier, own], axis=0)
+
+        tiles = [(g, i) for g in some for i in range(2)]
+        seen = [jnp.concatenate([allow[q, i] > 0.5] * GROUP, axis=0) for i in range(2)]
+        ones = jnp.ones((back + half, HEAD), BF)
         scores = [
             lax.dot_general(
-                qs[g, :, cols], keys, (((1,), (1,)), ((), ())), preferred_element_type=F32
+                jnp.concatenate([qs[g, parts[i], cols] for cols in heads], axis=0),
+                seen_rows(g, i, heads[0]),
+                (((1,), (1,)), ((), ())),
+                preferred_element_type=F32,
             )
-            for cols in heads
-        ]
-        scores = [jnp.where(seen, s * (1.0 / math.sqrt(HEAD)), NEGATIVE) for s in scores]
-        highest = [jnp.max(s, axis=1, keepdims=True) for s in scores]
-        weighted = [jnp.exp(s - m) for s, m in zip(scores, highest)]
-        totals = [jnp.sum(e, axis=1, keepdims=True) for e in weighted]
-        mixed = [jnp.dot(e.astype(BF), vals, preferred_element_type=F32) for e in weighted]
-        for cols, mix, total in zip(heads, mixed, totals):
-            result = jnp.where(alive, xin[q, g, :, cols].astype(F32) + mix / total, 0.0)
-            xin[q, g, :, cols] = result.astype(BF)
-
+            for g, i in tiles
+        ]
+        scores = [jnp.where(seen[i], a, NEGATIVE) for (_, i), a in zip(tiles, scores)]
+        highest = [jnp.max(a, axis=1, keepdims=True) for a in scores]
+        scale = math.log2(math.e) / math.sqrt(HEAD)
+        weighted = [jnp.exp2((a - m) * scale).astype(BF) for a, m in zip(scores, highest)]
+        mixed = [
+            jnp.dot(
+                e, jnp.concatenate([seen_rows(g, i, heads[1]), ones], axis=1),
+                preferred_element_type=F32,
+            )
+            for (g, i), e in zip(tiles, weighted)
+        ]
+        for (g, i), mix in zip(tiles, mixed):
+            mix = mix[:, :HEAD] / mix[:, HEAD:]
+            alive = live[q, parts[i]] > 0.5
+            for h, cols in enumerate(heads):
+                more = mix[h * half : (h + 1) * half]
+                result = jnp.where(alive, xin[q, g, parts[i], cols].astype(F32) + more, 0.0)
+                xin[q, g, parts[i], cols] = result.astype(BF)
+
+        for g in some:
+            send_on(s, q, g)
+
+    def send_on(s, q, g):
         @pl.when((s == 0) & (z < last_z))
         def _():
             relay(q, g).start()
@@ -332,29 +367,47 @@
         def _(g):
             relay(q, g).wait_recv()
 
-    @pl.loop(0, groups * works)
+    def layer(s, q):
+        norm(s, q)
+        for g in range(groups):
+            project_kv(s, q, g)
+        for g in range(groups):
+            project_q(s, g)
+
+        @pl.loop(0, groups // STEP)
+        def _(g):
+            attend(s, q, tuple(g * STEP + i for i in range(STEP)))
+
+    @pl.when(paired == 1)
+    def _():
+        handed[0].wait_recv()
+        handed[1].wait_recv()
+
+    @pl.loop(groups, groups + (groups - 1) * paired)
+    def _(g):
+        start(step1(g))
+
+    @pl.loop(0, first)
     def _(g):
         arrive(step1(g))
         start(step2(g))
-
-    @pl.when(paired == 1)
-    def _():
-        handed[0].wait_recv()
-
-        @pl.loop(groups, 2 * groups)
-        def _(g):
-            start(step1(g))
 
     def row_steps(g):
         arrive(step2(g))
         start(step3(g))
         start(share(g, 0))
 
-    @pl.loop(0, 2 * works)
+    @pl.loop(0, 2 * works + gives)
     def _(g):
         row_steps(g)
 
-    @pl.loop(0, blocks + works)
+    def finish(g):
+        arrive(step4(g))
+        start(share(g, 3))
+        for which in range(4):
+            arrive(share(g, which))
+
+    @pl.loop(0, blocks + 1)
     def _(i):
         @pl.when(i < blocks)
         def _():
@@ -375,10 +428,7 @@
         @pl.when(i > 0)
         def _():
             g = i - 1
-            arrive(step4(g))
-            start(share(g, 3))
-            for which in range(4):
-                arrive(share(g, which))
+            finish(g)
 
             @pl.when((z == 0) & (g == 0))
             def _():
@@ -389,11 +439,23 @@
             def _():
                 project_kv(0, 0, g)
                 project_q(0, g)
-                attend(0, 0, g)
+                attend(0, 0, (g,))
+
+    share_y = pl.ds(2 * c, 2)
+    whole = send(
+        wv.at[0, share_y], wv.at[2 * groups - 1, share_y], ws.at[2], wr.at[2], up(1, r)
+    )
+    half_whole = same(wv.at[2 * groups - 1, share_y], ws.at[3], wr.at[3], sibling)
+
+    @pl.when(gives == 1)
+    def _():
+        whole.start()
 
     @pl.when(paired == 1)
     def _():
-        handed[1].wait_recv()
+        whole.wait_recv()
+        half_whole.start()
+        half_whole.wait_recv()
 
     @pl.loop(1 - (z + last_z) // (last_z + 1), chunks * works)
     def _(q):
@@ -401,16 +463,7 @@
 
         @pl.loop(0, 1 + paired)
         def _(k):
-            s = paired - k
-            norm(s, q)
-            for g in range(groups):
-                project_kv(s, q, g)
-            for g in range(groups):
-                project_q(s, g)
-
-            @pl.loop(0, groups)
-            def _(g):
-                attend(s, q, g)
+            layer(paired - k, q)
 
     @pl.when(z < last_z)
     def _():
@@ -436,6 +489,11 @@
     @pl.when(gives == 1)
     def _():
         sent(handed)
+        whole.wait_send()
+
+    @pl.when(paired == 1)
+    def _():
+        half_whole.wait_send()
 
     @pl.loop(0, chunks)
     def _(q):
@@ -488,7 +546,7 @@
             pltpu.VMEM(doc_lengths.shape, jnp.int32),
             pltpu.VMEM(doc_shift.shape, jnp.int32),
             pltpu.SMEM(batch_lengths.shape, jnp.int32),
-            dma((5,)),
+            dma((groups + 4,)),
             pltpu.VMEM((2 * groups, NY, NX, 2, 2, 32, COLS), BF),
             state,
             pltpu.VMEM((rows, width), BF),
@@ -498,7 +556,7 @@
             pltpu.VMEM((2 * chunks, groups, rows, 2 * HEAD), BF),
             pltpu.VMEM((2 * chunks, groups, 1, rows, 2 * HEAD), BF),
             pltpu.VMEM((groups, rows, WIDE), BF),
-            pltpu.VMEM((chunks, rows, 2 * rows), F32),
+            pltpu.VMEM((chunks, 2, rows // 2, rows + rows // 2), F32),
             flags,
             flags,
             flags,
@@ -506,7 +564,7 @@
             ring, ring, ring, ring, ring, ring, ring, ring,
             dma((2, 2 * groups, 4)), dma((2, 2 * groups, 4)),
             tasks, tasks, piece, piece, piece, piece, piece, piece,
-            dma((2,)), dma((2,)), dma((1,)),
+            dma((4,)), dma((4,)), dma((1,)),
         ],
         compiler_params=pltpu.CompilerParams(
             collective_id=0, has_side_effects=True, vmem_limit_bytes=48 << 20

time: 178 us -> 175 us (0.983)
  Pallas kernels: 171 us -> 166 us
    pallas_call x1, Pallas kernels: 171 us -> 166 us  [shards(): pl.pallas_call(kernel, out_shape=jax.ShapeDtypeStruct((1, chunks, 2 * row...]
where the time goes in v4:
time: 175 us; the launch traced here: 173 us
  Pallas kernels  166 us (95%)
  local copies, waits for them, and re-layouts  6.51 us (4%)
    pallas_call x1, Pallas kernels, shards(): pl.pallas_call(kernel, out_shape=jax.ShapeDtypeStruct((1, chunks, 2 * row...  166 us
    unnamed x13, local copies, waits for them, and re-layouts  6.51 us

profile of v4, /device:TPU:240, one launch (start us, length us, event | category | flops | bytes accessed | tf_op | source)
XLA Modules:
  0.0 172.7 jit_solution(12996191613422953939)
XLA Ops:
  0.0 0.0 copy-start
  0.0 1.3 copy-done
  1.3 0.0 copy-start.1
  1.3 1.0 copy-done.1
  2.3 0.0 copy-start.2
  2.3 0.7 copy-done.2
  3.0 0.0 copy-start.3
  3.0 0.7 copy-done.3
  3.7 0.0 copy-start.4
  3.7 0.7 copy-done.4
  4.4 0.0 copy-start.5
  4.4 0.7 copy-done.5
  5.0 166.2 %relay.1 = bf16[1,2,320,2048]{3,2,1,0:T(8,128)(2,1)S(1)} custom-call(bf16[2,160,2048]{2,1,0:T(8,128)(2,1)S(1)} %copy-done, f32[1,2048]{1,0:T(1,128)S(1)} %copy-done.2, bf16[1,64,3072]{2,1,0:T(8,128)(2,1)S(1)} %copy-done.1, s32[2,128]{1,0:T(2,128)S(1)} %copy-done.3, s32[2,128]{1,0:T(2,128)S(1)} %copy-done.4, s32[2]{0:T(128)S(1)} %copy-done.5), custom_call_target="tpu_custom_call" | custom-call | tf_op jit(solution)/shard_map/relay/pallas_call | solution.py:539
  171.2 1.5 copy.8
Async XLA Ops:
  0.0 1.3 copy-start
  1.3 1.0 copy-start.1
  2.3 0.7 copy-start.2
  3.0 0.7 copy-start.3
  3.7 0.7 copy-start.4
  4.4 0.7 copy-start.5

commit v5 on v4

--- a/solution.py
+++ b/solution.py
@@ -184,37 +184,7 @@
     def _():
         handed[1].start()
 
-    spot = lax.broadcasted_iota(jnp.int32, (HEAD, HEAD), 0)
-    until = lax.broadcasted_iota(jnp.int32, (HEAD, HEAD), 1)
-    upto = jnp.where(spot <= until, 1.0, 0.0).astype(BF)
-    length = lens[...].astype(F32)
-    ends = jnp.dot(length.astype(BF), upto, preferred_element_type=F32)
-    starts = ends - length
-    moves = shifts[...].astype(F32)
-    base = (r * rows).astype(F32)
-    for q in range(chunks):
-        begin, end, move = starts[q : q + 1], ends[q : q + 1], moves[q : q + 1]
-        place = lax.broadcasted_iota(jnp.int32, (rows, HEAD), 0).astype(F32) + base
-        before, after = begin <= place, end > place
-        doc_start = jnp.max(jnp.where(before, begin, -1.0), axis=1, keepdims=True)
-        doc_end = jnp.min(jnp.where(after, end, 1e9), axis=1, keepdims=True)
-        shift = jnp.max(jnp.where(before & after, move, 0.0), axis=1, keepdims=True)
-        edge = base + rows
-        moved = (doc_start >= base) & (shift > 0.5) & (edge < float(rows) * ranks)
-        to_next = jnp.where((doc_end > edge) | moved, 1.0, 0.0)
-        alive = jnp.where(place < blen[q].astype(F32), 1.0, 0.0)
-        live[q] = alive
-        sel_a[q] = alive * (1.0 - to_next)
-        sel_b[q] = alive * to_next
-        for i in range(2):
-            part = slice(i * half, (i + 1) * half)
-            span = (half, back + half)
-            query = lax.broadcasted_iota(jnp.int32, span, 0).astype(F32) + (base + i * half)
-            key = lax.broadcasted_iota(jnp.int32, span, 1).astype(F32) + (base + i * half - back)
-            seen = (key >= doc_start[part]) & (key <= query)
-            allow[q, i] = jnp.where(seen, 1.0, 0.0)
-
-    @pl.when(r == 0)
+    @pl.when((r == 0) & (works == 1))
     def _():
         halo[...] = jnp.zeros_like(halo)
 
@@ -225,16 +195,6 @@
         return pltpu.make_async_copy(
             zero, out.at[0, q, pl.ds(0, rows), columns(g)], cleared.at[0]
         )
-
-    @pl.when(r == 0)
-    def _():
-        zero[...] = jnp.zeros_like(zero)
-
-        @pl.loop(0, chunks)
-        def _(q):
-            @pl.loop(0, groups)
-            def _(g):
-                blank(q, g).start()
 
     def norm(s, q):
         gains = gain[s]
@@ -395,26 +355,68 @@
     def row_steps(g):
         arrive(step2(g))
         start(step3(g))
-        start(share(g, 0))
+
+        @pl.when(works == 1)
+        def _():
+            start(share(g, 0))
+
 
     @pl.loop(0, 2 * works + gives)
     def _(g):
         row_steps(g)
 
+    spot = lax.broadcasted_iota(jnp.int32, (HEAD, HEAD), 0)
+    until = lax.broadcasted_iota(jnp.int32, (HEAD, HEAD), 1)
+    upto = jnp.where(spot <= until, 1.0, 0.0).astype(BF)
+    length = lens[...].astype(F32)
+    ends = jnp.dot(length.astype(BF), upto, preferred_element_type=F32)
+    starts = ends - length
+    moves = shifts[...].astype(F32)
+    base = (r * rows).astype(F32)
+    for q in range(chunks):
+        begin, end, move = starts[q : q + 1], ends[q : q + 1], moves[q : q + 1]
+        place = lax.broadcasted_iota(jnp.int32, (rows, HEAD), 0).astype(F32) + base
+        before, after = begin <= place, end > place
+        doc_start = jnp.max(jnp.where(before, begin, -1.0), axis=1, keepdims=True)
+        doc_end = jnp.min(jnp.where(after, end, 1e9), axis=1, keepdims=True)
+        shift = jnp.max(jnp.where(before & after, move, 0.0), axis=1, keepdims=True)
+        edge = base + rows
+        moved = (doc_start >= base) & (shift > 0.5) & (edge < float(rows) * ranks)
+        to_next = jnp.where((doc_end > edge) | moved, 1.0, 0.0)
+        alive = jnp.where(place < blen[q].astype(F32), 1.0, 0.0)
+        live[q] = alive
+        sel_a[q] = alive * (1.0 - to_next)
+        sel_b[q] = alive * to_next
+        for i in range(2):
+            part = slice(i * half, (i + 1) * half)
+            span = (half, back + half)
+            query = lax.broadcasted_iota(jnp.int32, span, 0).astype(F32) + (base + i * half)
+            key = lax.broadcasted_iota(jnp.int32, span, 1).astype(F32) + (base + i * half - back)
+            seen = (key >= doc_start[part]) & (key <= query)
+            allow[q, i] = jnp.where(seen, 1.0, 0.0)
+
     def finish(g):
         arrive(step4(g))
-        start(share(g, 3))
-        for which in range(4):
-            arrive(share(g, which))
-
-    @pl.loop(0, blocks + 1)
+
+        @pl.when(works == 1)
+        def _():
+            start(share(g, 3))
+            for which in range(4):
+                arrive(share(g, which))
+
+
+    @pl.loop(0, blocks + 2 - (z + last_z) // (last_z + 1))
     def _(i):
         @pl.when(i < blocks)
         def _():
             arrive(step3(i))
             start(step4(i))
-            start(share(i, 1))
-            start(share(i, 2))
+
+            @pl.when(works == 1)
+            def _():
+                start(share(i, 1))
+                start(share(i, 2))
+
 
             @pl.when(i + 2 < blocks)
             def _():
@@ -425,7 +427,11 @@
                 arrive(step1(i + groups))
                 start(step2(i + groups))
 
-        @pl.when(i > 0)
+        @pl.when((z == 0) & (i > 1))
+        def _():
+            attend(0, 0, (i - 2,))
+
+        @pl.when((i > 0) & (i <= blocks))
         def _():
             g = i - 1
             finish(g)
@@ -439,13 +445,11 @@
             def _():
                 project_kv(0, 0, g)
                 project_q(0, g)
-                attend(0, 0, (g,))
-
-    share_y = pl.ds(2 * c, 2)
+
     whole = send(
-        wv.at[0, share_y], wv.at[2 * groups - 1, share_y], ws.at[2], wr.at[2], up(1, r)
+        wv.at[0, :, :, c], wv.at[2 * groups - 1, :, :, c], ws.at[2], wr.at[2], up(1, r)
     )
-    half_whole = same(wv.at[2 * groups - 1, share_y], ws.at[3], wr.at[3], sibling)
+    half_whole = same(wv.at[2 * groups - 1, :, :, c], ws.at[3], wr.at[3], sibling)
 
     @pl.when(gives == 1)
     def _():
@@ -464,6 +468,16 @@
         @pl.loop(0, 1 + paired)
         def _(k):
             layer(paired - k, q)
+
+    @pl.when(r == 0)
+    def _():
+        zero[...] = jnp.zeros_like(zero)
+
+        @pl.loop(0, chunks)
+        def _(q):
+            @pl.loop(0, groups)
+            def _(g):
+                blank(q, g).start()
 
     @pl.when(z < last_z)
     def _():
@@ -483,8 +497,12 @@
         sent(step2(g))
         sent(step3(g))
         sent(step4(g))
-        for which in range(4):
-            sent(share(g, which))
+
+        @pl.when(works == 1)
+        def _():
+            for which in range(4):
+                sent(share(g, which))
+
 
     @pl.when(gives == 1)
     def _():

time: 175 us -> 172 us (0.983)
  Pallas kernels: 166 us -> 164 us
    pallas_call x1, Pallas kernels: 166 us -> 164 us  [shards(): pl.pallas_call(kernel, out_shape=jax.ShapeDtypeStruct((1, chunks, 2 * row...]
where the time goes in v5:
time: 172 us; the launch traced here: 171 us
  Pallas kernels  164 us (95%)
  local copies, waits for them, and re-layouts  6.51 us (4%)
    pallas_call x1, Pallas kernels, shards(): pl.pallas_call(kernel, out_shape=jax.ShapeDtypeStruct((1, chunks, 2 * row...  164 us
    unnamed x13, local copies, waits for them, and re-layouts  6.51 us

profile of v5, /device:TPU:240, one launch (start us, length us, event | category | flops | bytes accessed | tf_op | source)
XLA Modules:
  0.0 170.6 jit_solution(11070332669265916716)
XLA Ops:
  0.0 0.0 copy-start
  0.0 1.3 copy-done
  1.3 0.0 copy-start.1
  1.3 1.0 copy-done.1
  2.3 0.0 copy-start.2
  2.3 0.7 copy-done.2
  3.0 0.0 copy-start.3
  3.0 0.7 copy-done.3
  3.7 0.0 copy-start.4
  3.7 0.7 copy-done.4
  4.4 0.0 copy-start.5
  4.4 0.7 copy-done.5
  5.0 164.1 %relay.1 = bf16[1,2,320,2048]{3,2,1,0:T(8,128)(2,1)S(1)} custom-call(bf16[2,160,2048]{2,1,0:T(8,128)(2,1)S(1)} %copy-done, f32[1,2048]{1,0:T(1,128)S(1)} %copy-done.2, bf16[1,64,3072]{2,1,0:T(8,128)(2,1)S(1)} %copy-done.1, s32[2,128]{1,0:T(2,128)S(1)} %copy-done.3, s32[2,128]{1,0:T(2,128)S(1)} %copy-done.4, s32[2]{0:T(128)S(1)} %copy-done.5), custom_call_target="tpu_custom_call" | custom-call | tf_op jit(solution)/shard_map/relay/pallas_call | solution.py:557
  169.1 1.5 copy.8
Async XLA Ops:
  0.0 1.3 copy-start
  1.3 1.0 copy-start.1
  2.3 0.7 copy-start.2
  3.0 0.7 copy-start.3
  3.7 0.7 copy-start.4
  4.4 0.7 copy-start.5

commit v6 on v5

--- a/solution.py
+++ b/solution.py
@@ -208,7 +208,7 @@
             inverse = lax.rsqrt(total * (1.0 / width) + EPSILON)
             for g in range(groups):
                 cols = slice(g * WIDE, (g + 1) * WIDE)
-                xn[part, cols] = (values[g] * inverse * gains[:, cols]).astype(BF)
+                xn[q, part, cols] = (values[g] * inverse * gains[:, cols]).astype(BF)
 
     def halo_copy(t, g):
         return send(kv.at[t, g], halo.at[t, g, 0], hs.at[t, g], hr.at[t, g], (z, right))
@@ -246,18 +246,18 @@
         block = wv[slot(s, g), :, :, :, :, :, first : first + count]
         return block.reshape(width, count)
 
-    def project_kv(s, q, g):
+    def project_kv(s, q, g, held=0):
         t = s * chunks + q
         kv[t, g] = jnp.dot(
-            xn[...], weights(s, g, WIDE, 2 * HEAD), preferred_element_type=F32
+            xn[q], weights(s, g, WIDE, 2 * HEAD), preferred_element_type=F32
         ).astype(BF)
 
-        @pl.when(r < ranks - 1)
+        @pl.when((r < ranks - 1) & (held == 0))
         def _():
             halo_copy(t, g).start()
 
-    def project_q(s, g):
-        qs[g] = jnp.dot(xn[...], weights(s, g, 0, WIDE), preferred_element_type=F32).astype(BF)
+    def project_q(s, q, g):
+        qs[g] = jnp.dot(xn[q], weights(s, g, 0, WIDE), preferred_element_type=F32).astype(BF)
 
     heads = [slice(h * HEAD, (h + 1) * HEAD) for h in range(GROUP)]
     parts = [slice(i * half, (i + 1) * half) for i in range(2)]
@@ -328,11 +328,14 @@
             relay(q, g).wait_recv()
 
     def layer(s, q):
-        norm(s, q)
+        @pl.when(z > 0)
+        def _():
+            norm(s, q)
+            for g in range(groups):
+                project_kv(s, q, g)
+
         for g in range(groups):
-            project_kv(s, q, g)
-        for g in range(groups):
-            project_q(s, g)
+            project_q(s, q, g)
 
         @pl.loop(0, groups // STEP)
         def _(g):
@@ -438,13 +441,22 @@
 
             @pl.when((z == 0) & (g == 0))
             def _():
-                take(0)
-                norm(0, 0)
+                @pl.loop(0, chunks)
+                def _(q):
+                    take(q)
+                    norm(0, q)
 
             @pl.when(z == 0)
             def _():
                 project_kv(0, 0, g)
-                project_q(0, g)
+                project_q(0, 0, g)
+                project_kv(0, 1, g, 1)
+
+                @pl.when((g == groups - 1) & (r < ranks - 1))
+                def _():
+                    @pl.loop(0, groups)
+                    def _(k):
+                        halo_copy(1, k).start()
 
     whole = send(
         wv.at[0, :, :, c], wv.at[2 * groups - 1, :, :, c], ws.at[2], wr.at[2], up(1, r)
@@ -463,7 +475,9 @@
 
     @pl.loop(1 - (z + last_z) // (last_z + 1), chunks * works)
     def _(q):
-        take(q)
+        @pl.when(z > 0)
+        def _():
+            take(q)
 
         @pl.loop(0, 1 + paired)
         def _(k):
@@ -567,7 +581,7 @@
             dma((groups + 4,)),
             pltpu.VMEM((2 * groups, NY, NX, 2, 2, 32, COLS), BF),
             state,
-            pltpu.VMEM((rows, width), BF),
+            pltpu.VMEM((chunks, rows, width), BF),
             state,
             state,
             state,

time: 172 us -> 180 us (1.047)
  Pallas kernels: 164 us -> 172 us
    pallas_call x1, Pallas kernels: 164 us -> 172 us  [shards(): pl.pallas_call(kernel, out_shape=jax.ShapeDtypeStruct((1, chunks, 2 * row...]
where the time goes in v6:
time: 180 us; the launch traced here: 178 us
  Pallas kernels  172 us (96%)
  local copies, waits for them, and re-layouts  6.51 us (4%)
    pallas_call x1, Pallas kernels, shards(): pl.pallas_call(kernel, out_shape=jax.ShapeDtypeStruct((1, chunks, 2 * row...  172 us
    unnamed x13, local copies, waits for them, and re-layouts  6.51 us

profile of v6, /device:TPU:240, one launch (start us, length us, event | category | flops | bytes accessed | tf_op | source)
XLA Modules:
  0.0 178.4 jit_solution(6947219296112100292)
XLA Ops:
  0.0 0.0 copy-start
  0.0 1.3 copy-done
  1.3 0.0 copy-start.1
  1.3 1.0 copy-done.1
  2.3 0.0 copy-start.2
  2.3 0.7 copy-done.2
  3.0 0.0 copy-start.3
  3.0 0.7 copy-done.3
  3.7 0.0 copy-start.4
  3.7 0.7 copy-done.4
  4.4 0.0 copy-start.5
  4.4 0.7 copy-done.5
  5.0 171.9 %relay.1 = bf16[1,2,320,2048]{3,2,1,0:T(8,128)(2,1)S(1)} custom-call(bf16[2,160,2048]{2,1,0:T(8,128)(2,1)S(1)} %copy-done, f32[1,2048]{1,0:T(1,128)S(1)} %copy-done.2, bf16[1,64,3072]{2,1,0:T(8,128)(2,1)S(1)} %copy-done.1, s32[2,128]{1,0:T(2,128)S(1)} %copy-done.3, s32[2,128]{1,0:T(2,128)S(1)} %copy-done.4, s32[2]{0:T(128)S(1)} %copy-done.5), custom_call_target="tpu_custom_call" | custom-call | tf_op jit(solution)/shard_map/relay/pallas_call | solution.py:571
  176.9 1.5 copy.8
Async XLA Ops:
  0.0 1.3 copy-start
  1.3 1.0 copy-start.1
  2.3 0.7 copy-start.2
  3.0 0.7 copy-start.3
  3.7 0.7 copy-start.4
  4.4 0.7 copy-start.5
